TPU v7x, 256 devices: a whole 4x4x8 slice. The times are simulated.
256 devices in a mesh: dp: 2 (over core), seq: 16 (over x_hi, z), chan: 8 (over y, x_lo).
Axes of the slice: x: 4 (x_hi: 2, x_lo: 2; x = x_hi * 2 + x_lo), y: 4, z: 8, core: 2. Of those that a mesh axis runs over, the one named last changes fastest.
Arguments:
- recurrence_feed: bfloat16 [8192, 8192], P(('dp', 'seq'), 'chan'), parts along dimension 0, may hold values from -6 to 6
- memory_write_matrix: bfloat16 [8192, 128], P(('dp', 'seq')), parts along dimension 0, may hold values from -0.5 to 0.5
- memory_read_matrix: bfloat16 [8192, 128], P(('dp', 'seq')), parts along dimension 0, may hold values from -0.5 to 0.5
- log_shrink_table: float32 [8192, 128], P(('dp', 'seq'), 'chan'), parts along dimension 0, may hold values from -0.5 to 0
- skip_connection_scale: float32 [128], P('chan'), may hold values from 0.5 to 2
- specialist_choices: int32 [8192, 2], P(('dp', 'seq')), parts along dimension 0, may hold values from 0 to 15, as said below
- specialist_mixing_shares: bfloat16 [8192, 2], P(('dp', 'seq')), parts along dimension 0, may hold values from 0.19921875 to 1
- specialist_rescale_vector: float32 [8192], P('chan'), may hold values from 0.25 to 1.75
- specialist_switch_matrix: bfloat16 [8192, 12288], P('chan', 'seq'), may hold values from -0.0625 to 0.0625
- specialist_widen_matrix: bfloat16 [8192, 12288], P('chan', 'seq'), may hold values from -0.0625 to 0.0625
- specialist_contract_matrix: bfloat16 [12288, 8192], P('seq', 'chan'), may hold values from -0.0546875 to 0.0546875
- closing_rescale_vector: float32 [8192], replicated, may hold values from 0.5 to 1.5
- lexicon_matrix: bfloat16 [8192, 32768], P(None, ('seq', 'chan')), may hold values from -19.887378 to 19.887378
- softness_divisor: float32 [1], replicated, may hold values from 0.5 to 1
- picked_entry_offsets: int32 [512], P(('dp', 'seq')), parts along dimension 0, may hold values from 0 to 255
Outputs:
- layer_out: bfloat16 [8192, 8192], P(('dp', 'seq'), 'chan'), parts along dimension 0
- log_probs: float32 [512, 32768], P('dp', ('seq', 'chan')), parts along dimension 0
There are 2 independent parts, one for each index of `dp`. A program takes and returns all parts, laid end to end along the dimension named above; an argument that names none is the same for every part. Nothing has to cross between parts.
Inputs may be any that keep to these rules, and one draw needn't show every extreme that they name: `specialist_choices`: the two experts of a row differ. In each aligned block of 256 rows, expert 0 is named by at most 64 rows, and by exactly 64 rows in some block.
All inputs are finite; a program needn't handle non-finite values.
Results may differ from a plain program's by a relative error of at most 0.01.
Values may be sent and summed in bfloat16 or wider, within the bound.
A program may use at most 64 MiB of HBM per device.

v0:
```python
import jax
import jax.numpy as jnp
from jax import lax
from jax.sharding import PartitionSpec as P

GROUP = 256


def carried_in(x, axis, combine, identity):
    devices, here = (lax.axis_size(axis), lax.axis_index(axis))
    everything = jax.tree.map(lambda part: lax.all_gather(part, axis), x)
    start = jax.tree.map(
        lambda part, zero: jnp.broadcast_to(jnp.asarray(zero, part.dtype), part.shape), x, identity
    )

    def hop(k, before):
        reached = k < here
        new = combine(before, jax.tree.map(lambda part: part[k], everything))
        return jax.tree.map(lambda a, b: jnp.where(reached, a, b), new, before)

    return lax.fori_loop(0, devices, hop, start)


def joined(part, axis, combine):
    gathered = jax.tree.map(lambda a: lax.all_gather(a, axis), part)

    def take(source):
        return jax.tree.map(lambda a: lax.dynamic_index_in_dim(a, source, 0, False), gathered)

    return lax.fori_loop(
        1, lax.axis_size(axis), lambda source, state: combine(state, take(source)), take(0)
    )


def compose(earlier, later):
    return (earlier[0] * later[0], later[0][:, None, None] * earlier[1] + later[1])


def combine_totals(first, second):
    top_value = jnp.maximum(first[0], second[0])
    return (
        top_value,
        first[1] * jnp.exp(first[0] - top_value) + second[1] * jnp.exp(second[0] - top_value),
    )


def shards(
    recurrence_feed,
    memory_write_matrix,
    memory_read_matrix,
    log_shrink_table,
    skip_connection_scale,
    specialist_choices,
    specialist_mixing_shares,
    specialist_rescale_vector,
    specialist_switch_matrix,
    specialist_widen_matrix,
    specialist_contract_matrix,
    closing_rescale_vector,
    lexicon_matrix,
    softness_divisor,
    picked_entry_offsets,
):
    shard_len, chan_width = recurrence_feed.shape
    head_count = log_shrink_table.shape[1]
    head_dim = chan_width // head_count
    state_dim = memory_write_matrix.shape[1]
    block_count = shard_len // GROUP
    chan_count = lax.axis_size("chan")
    capacity = shard_len // 4
    model_width = chan_width * chan_count
    x_blocks = recurrence_feed.reshape(block_count, GROUP, head_count, head_dim)
    b_blocks = memory_write_matrix.reshape(block_count, GROUP, state_dim)
    c_blocks = memory_read_matrix.reshape(block_count, GROUP, state_dim)
    cumulative = jnp.cumsum(log_shrink_table.reshape(block_count, GROUP, head_count), axis=1)
    scores = jnp.einsum("kin,kjn->kij", c_blocks, b_blocks, preferred_element_type=jnp.float32)
    causal = jnp.arange(GROUP)[:, None] >= jnp.arange(GROUP)[None, :]
    spread = cumulative[:, :, None, :] - cumulative[:, None, :, :]
    decay_mat = jnp.where(causal[None, :, :, None], jnp.exp(jnp.minimum(spread, 0.0)), 0.0)
    mixing = (scores[..., None] * decay_mat).astype(jnp.bfloat16)
    y_inner = jnp.einsum("kijh,kjhp->kihp", mixing, x_blocks, preferred_element_type=jnp.float32)
    tail_decay = jnp.exp(cumulative[:, -1:, :] - cumulative)
    weighted = (x_blocks.astype(jnp.float32) * tail_decay[..., None]).astype(jnp.bfloat16)
    local_state = jnp.einsum(
        "kjhp,kjn->khpn", weighted, b_blocks, preferred_element_type=jnp.float32
    )
    block_decay = jnp.exp(cumulative[:, -1, :])
    prefix_state = jnp.zeros((head_count, head_dim, state_dim), jnp.float32)
    prefix_decay = jnp.ones((head_count,), jnp.float32)
    prefix_list = prefix_state
    decay_list = prefix_decay
    prefix_state = block_decay[0][:, None, None] * prefix_state + local_state[0]
    prefix_decay = prefix_decay * block_decay[0]
    identity = (
        jnp.ones((head_count,), jnp.float32),
        jnp.zeros((head_count, head_dim, state_dim), jnp.float32),
    )
    entry_pair = carried_in((prefix_decay, prefix_state), "seq", compose, identity)
    entry_state = entry_pair[1]
    starts = jnp.stack([decay_list[:, None, None] * entry_state + prefix_list])
    y_outer = jnp.exp(cumulative)[..., None] * jnp.einsum(
        "kin,khpn->kihp", c_blocks.astype(jnp.float32), starts, precision=lax.Precision.HIGHEST
    )
    mamba_out = (
        y_inner
        + y_outer
        + skip_connection_scale[None, None, :, None] * x_blocks.astype(jnp.float32)
    )
    mamba_out = mamba_out.astype(jnp.bfloat16).reshape(shard_len, chan_width)
    chosen = specialist_choices == 0
    token_used = jnp.any(chosen, axis=1)
    gate_sum = jnp.sum(jnp.where(chosen, specialist_mixing_shares.astype(jnp.float32), 0.0), axis=1)
    place = jnp.cumsum(token_used.astype(jnp.int32)) - 1
    slot_map = (place[:, None] == jnp.arange(capacity, dtype=jnp.int32)[None, :]) & token_used[
        :, None
    ]
    slot_buffer = jnp.einsum(
        "tc,td->cd", slot_map.astype(jnp.bfloat16), mamba_out, preferred_element_type=jnp.float32
    ).astype(jnp.bfloat16)
    slot_rows = lax.all_gather(slot_buffer, "seq", axis=0, tiled=True)
    values = slot_rows.astype(jnp.float32)
    total_squares = lax.psum(jnp.sum(values * values, axis=-1), "chan")
    inv_rms = lax.rsqrt(total_squares / model_width + 1e-05)
    normed = (values * inv_rms[:, None] * specialist_rescale_vector).astype(jnp.bfloat16)
    gate_part = jnp.dot(normed, specialist_switch_matrix, preferred_element_type=jnp.float32)
    up_part = jnp.dot(normed, specialist_widen_matrix, preferred_element_type=jnp.float32)
    gate_total, up_total = (
        lax.psum(gate_part.astype(jnp.bfloat16), "chan").astype(jnp.float32),
        lax.psum(up_part.astype(jnp.bfloat16), "chan").astype(jnp.float32),
    )
    hidden = (jax.nn.silu(gate_total) * up_total).astype(jnp.bfloat16)
    expert_out = jnp.dot(hidden, specialist_contract_matrix, preferred_element_type=jnp.float32)
    returned = lax.psum_scatter(
        expert_out.astype(jnp.bfloat16), "seq", scatter_dimension=0, tiled=True
    ).astype(jnp.float32)
    slot_of_token = jnp.clip(place, 0, capacity - 1)
    contrib = jnp.take(returned, slot_of_token, axis=0)
    scale = jnp.where(token_used, gate_sum, 0.0)
    layer_out = (mamba_out.astype(jnp.float32) + scale[:, None] * contrib).astype(jnp.bfloat16)
    picked = jnp.take(layer_out, picked_entry_offsets, axis=0)
    full_rows = lax.all_gather(picked, "chan", axis=1, tiled=True).astype(jnp.float32)
    row_rms = lax.rsqrt(jnp.mean(full_rows * full_rows, axis=-1, keepdims=True) + 1e-05)
    normed_rows = (full_rows * row_rms * closing_rescale_vector).astype(jnp.bfloat16)
    lexicon_scores = jnp.dot(
        lax.all_gather(normed_rows, "seq", axis=0, tiled=True),
        lexicon_matrix,
        preferred_element_type=jnp.float32,
    )
    softened_scores = lexicon_scores / softness_divisor[0]
    row_peak = jnp.max(softened_scores, axis=1)
    row_mass = jnp.sum(jnp.exp(softened_scores - row_peak[:, None]), axis=1)
    global_peak, global_mass = joined((row_peak, row_mass), ("seq", "chan"), combine_totals)
    log_probs = softened_scores - global_peak[:, None] - jnp.log(global_mass)[:, None]
    return (layer_out, log_probs)


def solution(mesh):
    in_specs = (
        P(("dp", "seq"), "chan"),
        P(("dp", "seq"), None),
        P(("dp", "seq"), None),
        P(("dp", "seq"), "chan"),
        P("chan"),
        P(("dp", "seq"), None),
        P(("dp", "seq"), None),
        P("chan"),
        P("chan", "seq"),
        P("chan", "seq"),
        P("seq", "chan"),
        P(),
        P(None, ("seq", "chan")),
        P(),
        P(("dp", "seq")),
    )
    out_specs = (P(("dp", "seq"), "chan"), P("dp", ("seq", "chan")))
    return jax.shard_map(shards, mesh=mesh, in_specs=in_specs, out_specs=out_specs, check_vma=False)
```

profile of v0, /device:TPU:2, one launch (start us, length us, event | category | flops | bytes accessed | tf_op | source)
XLA Modules:
  0.0 1476.3 jit_solution(15853400060192934747)
XLA Ops:
  7.3 0.8 copy_bitcast_fusion.2
  8.1 0.6 reduce-window.15
  8.7 0.2 slice_reduce_fusion
  8.8 0.1 copy.52
  9.1 0.1 copy.58
  9.1 1.3 copy.55
  10.4 0.1 fusion.23
  10.5 1.1 convolution_add_fusion
  11.7 0.1 copy.56
  11.8 0.1 copy.53
  11.9 0.3 reduce-window.19
  12.2 0.1 slice.22
  12.3 42.7 %all-gather = f32[16,1,16]{2,1,0:T(1,128)S(1)} all-gather(f32[1,1,16]{2,1,0:T(1,128)S(1)} %get-tuple-element.296), channel_id=2, replica_groups=mesh['dp'=2,'seq'=16,'chan'=8] {'seq'}, dimensions={0}, use_global_device_ids=true | all-gather | bytes 1088 | tf_op jit(solution)/shard_map/all_gather | solution.py:11
  55.0 0.1 slice_reduce_fusion.1
  55.2 0.1 compare_and_fusion.1
  55.3 0.2 fusion.43
  55.5 94.0 %all-gather.14.cloned.1.call-done = f32[256,64,128]{2,1,0:T(8,128)} async-done(((f32[16,64,128]{2,1,0:T(8,128)}), f32[256,64,128]{2,1,0:T(8,128)}) %all-gather.14.cloned.1.call-update) | async-done | bytes 8388624 | tf_op jit(solution)/shard_map/all_gather | solution.py:11
  149.5 19.4 %while.32 = (s32[]{:T(128)}, f32[16,64,128]{2,1,0:T(8,128)S(1)}, s32[]{:T(128)}, f32[16,16]{1,0:T(8,128)S(1)}, f32[16,16,64,128]{3,2,1,0:T(8,128)}, /*index=5*/s32[]{:T(128)}, s32[]{:T(128)}) while((s32[]{:T(128)}, f32[16,64,128]{2,1,0:T(8,128)S(1)}, s32[]{:T(128)}, f32[16,16]{1,0:T(8,128)S(1)}, f32[16,16,64,128]{3,2,1,0:T(8,128)}, ...), condition=%wide.region_3.4_spmd.clone, body=%wide.region_2.3_spmd.clone.sunk | while | flops 524292 | bytes 1573161 | solution.py:21
  149.5 1.2 fusion.57
  150.7 1.2 fusion.57
  151.9 1.2 fusion.57
  153.1 1.2 fusion.57
  154.3 1.2 fusion.57
  155.6 1.2 fusion.57
  156.8 1.2 fusion.57
  158.0 1.2 fusion.57
  159.2 1.2 fusion.57
  160.4 1.2 fusion.57
  161.6 1.2 fusion.57
  162.8 1.2 fusion.57
  164.0 1.2 fusion.57
  165.3 1.2 fusion.57
  166.5 1.2 fusion.57
  167.7 1.2 fusion.57
  168.9 0.6 fusion.19
  169.5 1.5 fusion.22
  171.0 1.1 convolution_convert_fusion.3
  172.1 0.0 all-reduce.3.cloned.1.call-start
  172.2 82.4 %all-gather.10.cloned.1.call-done = bf16[1024,1024]{1,0:T(8,128)(2,1)} async-done(((bf16[64,1024]{1,0:T(8,128)(2,1)}), bf16[1024,1024]{1,0:T(8,128)(2,1)}) %all-gather.10.cloned.1.call-update) | async-done | bytes 2097168 | tf_op jit(solution)/shard_map/all_gather | solution.py:120
  254.6 2.1 fusion.1
  256.7 17.6 %psum.21 = f32[1024]{0:T(1024)S(1)} all-reduce(f32[1024]{0:T(1024)S(1)} %fusion.1), channel_id=1, replica_groups=mesh['dp'=2,'seq'=16,'chan'=8] {'chan'}, use_global_device_ids=true, to_apply=%region_9.10 | all-reduce | flops 1024 | bytes 8192 | tf_op jit(solution)/shard_map/psum | solution.py:122
  274.3 5.2 convolution_convert_fusion.2
  279.5 3.0 convolution_convert_fusion.1
  282.6 145.5 %all-reduce.3.cloned.1.call-done = (bf16[1024,768]{1,0:T(8,128)(2,1)}, bf16[1024,768]{1,0:T(8,128)(2,1)}) async-done(((bf16[1024,768]{1,0:T(8,128)(2,1)}, bf16[1024,768]{1,0:T(8,128)(2,1)}), (bf16[1024,768]{1,0:T(8,128)(2,1)}, bf16[1024,768]{1,0:T(8,128)(2,1)})) %all-reduce.3.cloned.1.call-update) | async-done | bytes 3145744 | tf_op jit(solution)/shard_map/psum | solution.py:129
  428.1 5.3 convolution_convert_fusion
  433.5 0.0 all-gather.12.cloned.1.call-start
  433.5 0.1 fusion.36
  433.7 0.2 copy.59
  433.9 207.5 %reduce-scatter.2.cloned.1.call-done = bf16[64,1024]{1,0:T(8,128)(2,1)} async-done(((bf16[1024,1024]{1,0:T(8,128)(2,1)}), bf16[64,1024]{1,0:T(8,128)(2,1)}) %reduce-scatter.2.cloned.1.call-update) | async-done | bytes 131088 | tf_op jit(solution)/shard_map/reduce_scatter | solution.py:133
  641.4 0.9 convert_element_type.112
  642.3 1.1 gather_fusion
  643.4 1.0 add_convert_fusion
  644.5 1.7 gather_fusion.1
  646.2 0.1 broadcast_select_fusion
  646.3 28.8 %all_gather.31 = bf16[16,8192]{1,0:T(8,128)(2,1)S(1)} all-gather(bf16[16,1024]{1,0:T(8,128)(2,1)S(1)} %broadcast_select_fusion), channel_id=1, replica_groups=mesh['dp'=2,'seq'=16,'chan'=8] {'chan'}, dimensions={1}, use_global_device_ids=true | all-gather | bytes 294912 | tf_op jit(solution)/shard_map/all_gather | solution.py:141
  675.1 0.2 fusion.26
  675.3 0.8 fusion.28
  676.8 97.2 %all-gather.12.cloned.1.call-done = bf16[256,8192]{1,0:T(8,128)(2,1)} async-done(((bf16[16,8192]{1,0:T(8,128)(2,1)}), bf16[256,8192]{1,0:T(8,128)(2,1)}) %all-gather.12.cloned.1.call-update) | async-done | bytes 4194320 | tf_op jit(solution)/shard_map/all_gather | solution.py:145
  773.9 5.2 fusion.42
  779.2 0.1 exponential_reduce_fusion
  779.2 339.4 %all-gather.5 = f32[128,1,256]{2,1,0:T(1,128)S(1)} all-gather(f32[1,1,256]{2,1,0:T(1,128)S(1)} %bitcast.129), channel_id=5, replica_groups=mesh['dp'=2,'seq'=16,'chan'=8] {'seq','chan'}, dimensions={0}, use_global_device_ids=true | all-gather | bytes 132096 | tf_op jit(solution)/shard_map/all_gather | solution.py:25
  1118.7 342.8 %all-gather.4 = f32[128,1,256]{2,1,0:T(1,128)S(1)} all-gather(f32[1,1,256]{2,1,0:T(1,128)S(1)} %bitcast.128), channel_id=4, replica_groups=mesh['dp'=2,'seq'=16,'chan'=8] {'seq','chan'}, dimensions={0}, use_global_device_ids=true | all-gather | bytes 132096 | tf_op jit(solution)/shard_map/all_gather | solution.py:25
  1461.5 7.4 while.31
  1468.9 0.8 copy.60
  (327 shorter events, 4.8 us)
Async XLA Ops:
  7.2 421.0 %copy-start = (bf16[768,1024]{1,0:T(8,128)(2,1)S(1)}, bf16[768,1024]{1,0:T(8,128)(2,1)}, u32[]{:S(2)}) copy-start(bf16[768,1024]{1,0:T(8,128)(2,1)} %param.29) | copy-start | bytes 4718596
  7.2 3.3 copy-start.2
  7.2 4.6 copy-start.5
  7.2 48.1 %copy-start.3 = (bf16[256,128]{1,0:T(8,128)(2,1)S(1)}, bf16[256,128]{1,0:T(8,128)(2,1)}, u32[]{:S(2)}) copy-start(bf16[256,128]{1,0:T(8,128)(2,1)} %param.21) | copy-start | bytes 196612
  7.2 142.3 %all-gather.14.cloned.1.call-start = ((), (), s32[]{:S(2)}) async-start(), calls=%async_computation.4 | async-start | bytes 8912896 | tf_op jit(solution)/shard_map/all_gather | solution.py:11
  11.6 243.0 %all-gather.10.cloned.1.call-start = ((), (), s32[]{:S(2)}) async-start(), calls=%async_computation.1 | async-start | bytes 2228224 | tf_op jit(solution)/shard_map/all_gather | solution.py:120
  149.5 20.0 %copy-start.9 = (f32[16]{0:T(128)S(1)}, f32[16]{0:T(128)}, u32[]{:S(2)}) copy-start(f32[16]{0:T(128)} %param.23) | copy-start | bytes 196
  169.5 104.8 %copy-start.8 = (f32[1024]{0:T(1024)S(1)}, f32[1024]{0:T(1024)}, u32[]{:S(2)}) copy-start(f32[1024]{0:T(1024)} %param.26) | copy-start | bytes 12292
  172.1 256.0 %all-reduce.3.cloned.1.call-start = ((), (), s32[]{:S(2)}) async-start(), calls=%async_computation.5 | async-start | bytes 6291456 | tf_op jit(solution)/shard_map/psum | solution.py:129
  274.2 5.3 copy-start.1
  274.3 5.3 copy-start.7
  282.6 358.8 %reduce-scatter.2.cloned.1.call-start = ((), (), s32[]{:S(2)}) async-start(), calls=%async_computation.2 | async-start | bytes 2228224 | tf_op jit(solution)/shard_map/reduce_scatter | solution.py:133
  428.1 5.5 copy-start.10
  428.1 5.5 copy-start.6
  433.5 340.5 %all-gather.12.cloned.1.call-start = ((), (), s32[]{:S(2)}) async-start(), calls=%async_computation.3 | async-start | bytes 4456448 | tf_op jit(solution)/shard_map/all_gather | solution.py:145
  642.3 32.9 %copy-start.4 = (f32[8192]{0:T(1024)S(1)}, f32[8192]{0:T(1024)}, u32[]{:S(2)}) copy-start(f32[8192]{0:T(1024)} %param.30) | copy-start | bytes 98308
Sparse Core Ops, SparseCore 0:
  11.7 137.6 all-gather.13
  172.2 82.3 all-gather.9
  282.7 145.4 all-reduce.2
  433.6 207.7 reduce-scatter.1
  676.3 97.6 all-gather.11
where the time goes:
time: 1480 us
  blocking collectives  771 us (52%)
  waiting for transfers between devices  627 us (42%)
  other arithmetic  28 us (2%)
  matrix products  23.2 us (2%)
    all_gather x2, blocking collectives, joined(): gathered = jax.tree.map(lambda a: lax.all_gather(a, axis), part)  682 us
    reduce_scatter x1, waiting for transfers between devices, shards(): lax.psum_scatter(expert_out.astype(jnp.bfloat16), 'seq', scatter_dimensio...  208 us
    psum x1, waiting for transfers between devices, shards(): lax.psum(up_part.astype(jnp.bfloat16), 'chan').astype(jnp.float32)  146 us
    all_gather x1, waiting for transfers between devices, shards(): lax.all_gather(normed_rows, 'seq', axis=0, tiled=True)  97.2 us
    all_gather x1, waiting for transfers between devices, carried_in(): everything = jax.tree.map(lambda part: lax.all_gather(part, axis), x)  94 us
    all_gather x1, waiting for transfers between devices, shards(): slot_rows = lax.all_gather(slot_buffer, 'seq', axis=0, tiled=True)  82.4 us
    all_gather x1, blocking collectives, carried_in(): everything = jax.tree.map(lambda part: lax.all_gather(part, axis), x)  42.7 us
  transfers between devices with their start and end apart: 5, of which 5 were waited for; matrix products, arithmetic and copies ran while one was open for 0% of the time, Pallas kernels for 0%

commit v1 on v0

v1 whole, which is shorter than its diff:
```python
import jax
import jax.numpy as jnp
from jax import lax
from jax.experimental import pallas as pl
from jax.experimental.pallas import tpu as pltpu
from jax.sharding import PartitionSpec as P

MESH = pl.DeviceIdType.MESH
F32 = jnp.float32
BF16 = jnp.bfloat16
TOK = 256
CH = 1024
SEQ = 16
CHAN = 8
NZ = 8
CAP = 64
HIDL = 768
RSW = 2 * HIDL + 128
WIDTH = 8192
EPS = 1e-5
VMEM_LIMIT = 56 * 1024 * 1024


def dot(a, b):
    return jnp.dot(a, b, preferred_element_type=F32)


def split2(v):
    hi = v.astype(BF16)
    return hi, (v - hi.astype(F32)).astype(BF16)


def split3(v):
    hi = v.astype(BF16)
    rest = v - hi.astype(F32)
    mid = rest.astype(BF16)
    return hi, mid, (rest - mid.astype(F32)).astype(BF16)


def iota(shape, dim):
    return lax.broadcasted_iota(jnp.int32, shape, dim)


def remote(src, dst, send_sem, recv_sem, where):
    return pltpu.make_async_remote_copy(
        src_ref=src,
        dst_ref=dst,
        send_sem=send_sem,
        recv_sem=recv_sem,
        device_id=where,
        device_id_type=MESH,
    )


def greet(axis, size, me):
    barrier = pltpu.get_barrier_semaphore()

    def one(d, carry):
        pl.semaphore_signal(
            barrier, inc=1, device_id={axis: lax.rem(me + d, size)}, device_id_type=MESH
        )
        return carry

    lax.fori_loop(1, size, one, 0)


def scan_kernel(
    x_ref, b_ref, c_ref, la_ref, skip_ref, choice_ref, share_ref,
    mamba_ref, slots_ref, gmap_ref,
    wide, local, taken, decays, prefixes, entry, y_ref,
    dec_send, dec_recv, a_send, a_recv, p_send, p_recv,
):
    me = lax.axis_index("seq")
    greet("seq", SEQ, me)

    wide[...] = jnp.zeros_like(wide)
    wide[0:TOK, 0:16] = la_ref[...]
    wide[TOK : TOK + 1, 0:16] = skip_ref[...]
    tril = (iota((TOK, TOK), 0) >= iota((TOK, TOK), 1)).astype(F32)
    tril_bf = tril.astype(BF16)
    hi, mid, lo = split3(wide[0:TOK, :])
    cum = dot(tril_bf, hi) + dot(tril_bf, mid) + dot(tril_bf, lo)
    last = cum[TOK - 1 : TOK, :]
    spread_map = (iota((128, CH), 1) // 64 == iota((128, CH), 0)).astype(F32).astype(BF16)

    def expand(v):
        hi, lo = split2(v)
        return dot(hi, spread_map) + dot(lo, spread_map)

    decays[me] = jnp.broadcast_to(jnp.exp(last), (8, 128))
    pl.semaphore_wait(pltpu.get_barrier_semaphore(), SEQ - 1)

    def dec_copy(d, there):
        return remote(
            decays.at[me], decays.at[me], dec_send.at[d], dec_recv.at[d], {"seq": there}
        )

    def send_dec(d, carry):
        dec_copy(d, lax.rem(me + d, SEQ)).start()
        return carry

    lax.fori_loop(1, SEQ, send_dec, 0)

    weighted = (x_ref[...].astype(F32) * expand(jnp.exp(last - cum))).astype(BF16)
    b_t = jnp.transpose(b_ref[...].astype(F32)).astype(BF16)
    local[...] = dot(b_t, weighted).astype(BF16)

    def part(ref, p):
        return ref.at[
            pl.ds(pl.multiple_of((p // 2) * 16, 16), 16),
            pl.ds(pl.multiple_of((p % 2) * 512, 512), 512),
        ]

    def a_copy(d, there):
        return remote(part(local, there), taken.at[me], a_send.at[d], a_recv.at[d], {"seq": there})

    def send_a(d, carry):
        a_copy(d, lax.rem(me + d, SEQ)).start()
        return carry

    lax.fori_loop(1, SEQ, send_a, 0)
    taken[me] = part(local, me)[...]

    scores = lax.dot_general(
        c_ref[...], b_ref[...], (((1,), (1,)), ((), ())), preferred_element_type=F32
    )
    scores = scores * tril
    cum_t = jnp.transpose(cum)
    lane = iota((128, 128), 1)

    def heads(pairs):
        for q in pairs:
            cols = slice(128 * q, 128 * q + 128)
            xq = x_ref[:, cols]
            for r in range(2):
                rows = slice(128 * r, 128 * r + 128)
                width = 128 * (r + 1)
                out = []
                for h in (2 * q, 2 * q + 1):
                    decay = jnp.exp(
                        jnp.minimum(cum[rows, h : h + 1] - cum_t[h : h + 1, 0:width], 0.0)
                    )
                    mixing = (scores[rows, 0:width] * decay).astype(BF16)
                    out.append(dot(mixing, xq[0:width, :]))
                y_ref[rows, cols] = jnp.where(lane < 64, out[0], out[1])

    heads(range(0, 4))

    def wait_dec(d, carry):
        dec_copy(d, me).wait_recv()
        a_copy(d, me).wait_recv()
        return carry

    lax.fori_loop(1, SEQ, wait_dec, 0)
    half = lax.rem(me, 2)
    half_map = (
        ((iota((128, 512), 1) + half * 512) // 64 == iota((128, 512), 0)).astype(F32).astype(BF16)
    )
    hi, mid, lo = split3(decays[...].reshape(SEQ * 8, 128))
    factors = dot(hi, half_map) + dot(mid, half_map) + dot(lo, half_map)
    state = jnp.zeros((16, 512), F32)
    for s in range(SEQ):
        prefixes[s] = state.astype(BF16)
        state = factors[8 * s : 8 * s + 1, :] * state + taken[s].astype(F32)

    def p_copy(d, there):
        return remote(prefixes.at[there], part(entry, me), p_send.at[d], p_recv.at[d], {"seq": there})

    def send_p(d, carry):
        p_copy(d, lax.rem(me + d, SEQ)).start()
        return carry

    lax.fori_loop(1, SEQ, send_p, 0)
    part(entry, me)[...] = prefixes[me]

    heads(range(4, 8))

    first, second = choice_ref[:, 0:1] == 0, choice_ref[:, 1:2] == 0
    used = jnp.where(first, 1.0, 0.0) + jnp.where(second, 1.0, 0.0)
    gate = jnp.where(first, share_ref[:, 0:1].astype(F32), 0.0) + jnp.where(
        second, share_ref[:, 1:2].astype(F32), 0.0
    )
    used = jnp.broadcast_to(used, (TOK, 128))
    place = dot(tril_bf, used.astype(BF16)) - 1.0
    slot_map = jnp.where(place == iota((TOK, 128), 1).astype(F32), used, 0.0)
    gmap_ref[...] = (slot_map * gate).astype(BF16)
    slot_t = jnp.transpose(slot_map)[0:CAP, :].astype(BF16)

    skip_wide = expand(wide[TOK : TOK + 8, :])[0:1, :]
    cum_wide = expand(jnp.exp(cum))

    def wait_p(d, carry):
        there = lax.rem(me - d + SEQ, SEQ)
        remote(
            prefixes.at[me], part(entry, there), p_send.at[d], p_recv.at[d], {"seq": there}
        ).wait_recv()
        return carry

    lax.fori_loop(1, SEQ, wait_p, 0)
    outer = dot(c_ref[...], entry[...])
    mamba = (y_ref[...] + cum_wide * outer + skip_wide * x_ref[...].astype(F32)).astype(BF16)
    mamba_ref[...] = mamba
    slots_ref[...] = dot(slot_t, mamba).astype(BF16)

    def wait_sends(d, carry):
        dec_copy(d, me).wait_send()
        a_copy(d, me).wait_send()
        p_copy(d, me).wait_send()
        return carry

    lax.fori_loop(1, SEQ, wait_sends, 0)


def scan_call(*args):
    vm = pl.BlockSpec(memory_space=pltpu.VMEM)
    dma = pltpu.SemaphoreType.DMA
    return pl.pallas_call(
        scan_kernel,
        out_shape=(
            jax.ShapeDtypeStruct((TOK, CH), BF16),
            jax.ShapeDtypeStruct((CAP, CH), BF16),
            jax.ShapeDtypeStruct((TOK, 128), BF16),
        ),
        in_specs=[vm] * len(args),
        out_specs=(vm, vm, vm),
        scratch_shapes=[
            pltpu.VMEM((TOK + 8, 128), F32),
            pltpu.VMEM((128, CH), BF16),
            pltpu.VMEM((SEQ, 16, 512), BF16),
            pltpu.VMEM((SEQ, 8, 128), F32),
            pltpu.VMEM((SEQ, 16, 512), BF16),
            pltpu.VMEM((128, CH), BF16),
            pltpu.VMEM((TOK, CH), F32),
        ]
        + [dma((SEQ,))] * 6,
        compiler_params=pltpu.CompilerParams(
            collective_id=0, has_side_effects=True, vmem_limit_bytes=VMEM_LIMIT
        ),
        name="scan",
    )(*args)


def near_first(i):
    odd = i % 2
    return odd * ((i + 1) // 2) + (1 - odd) * ((NZ - i // 2) % NZ)


def expert_kernel(
    slots_ref, rescale_ref, switch_ref, widen_ref, contract_ref,
    out_ref,
    rows, parts, sums, hidden, x_out, x_in, kept, z_out, z_in,
    ag_send, ag_recv, fw_send, fw_recv, rs_send, rs_recv, hd_send, hd_recv,
    xs_send, xs_recv, zs_send, zs_recv,
):
    me = lax.axis_index("seq")
    ch = lax.axis_index("chan")
    xh, z = me // NZ, me % NZ
    other = (1 - xh) * NZ + z
    barrier = pltpu.get_barrier_semaphore()

    def greet_z(d, carry):
        pl.semaphore_signal(
            barrier, inc=1, device_id={"seq": xh * NZ + (z + d) % NZ}, device_id_type=MESH
        )
        return carry

    lax.fori_loop(1, NZ, greet_z, 0)
    pl.semaphore_signal(barrier, inc=1, device_id={"seq": other}, device_id_type=MESH)
    greet("chan", CHAN, ch)
    rows[me] = slots_ref[...]
    pl.semaphore_wait(barrier, 7 + 1 + 7)

    def ag_copy(d, src, there):
        return remote(rows.at[src], rows.at[src], ag_send.at[d], ag_recv.at[d], {"seq": there})

    def fw_copy(b, half):
        src = half * NZ + b
        return remote(rows.at[src], rows.at[src], fw_send.at[b], fw_recv.at[b], {"seq": other})

    fw_copy(z, xh).start()

    def send_ag(i, carry):
        d = near_first(i)
        ag_copy(d, me, xh * NZ + (z + d) % NZ).start()
        return carry

    lax.fori_loop(1, NZ, send_ag, 0)

    def forward(i):
        d = near_first(i)
        b = (z - d + NZ) % NZ
        ag_copy(d, xh * NZ + b, other).wait_recv()
        fw_copy(b, xh).start()

    def rs_copy(b, d, there, source):
        take = pl.ds(pl.multiple_of(there * 16, 16), 16)
        return remote(
            parts.at[b, take], sums.at[b, source], rs_send.at[b, d], rs_recv.at[b, d], {"chan": there}
        )

    def project(i, carry):
        @pl.when(i < NZ - 1)
        def _():
            forward(i + 1)

        b = (z - near_first(i) + NZ) % NZ
        fw_copy(b, 1 - xh).wait_recv()
        v = jnp.concatenate([rows[b], rows[NZ + b]], axis=0).astype(F32)
        squares = jnp.sum(v * v, axis=1, keepdims=True)
        scaled = (v * rescale_ref[...]).astype(BF16)
        parts[b, :, 0:HIDL] = dot(scaled, switch_ref[...]).astype(BF16)
        parts[b, :, HIDL : 2 * HIDL] = dot(scaled, widen_ref[...]).astype(BF16)
        hi, mid, lo = split3(squares)
        lane = iota((128, 128), 1)
        parts[b, :, 2 * HIDL :] = jnp.where(
            lane == 0,
            hi.astype(F32),
            jnp.where(lane == 1, mid.astype(F32), jnp.where(lane == 2, lo.astype(F32), 0.0)),
        ).astype(BF16)
        for d in range(1, CHAN):
            rs_copy(b, d, lax.rem(ch + d, CHAN), ch).start()
        return carry

    lax.fori_loop(0, NZ, project, 0)

    mine = pl.ds(pl.multiple_of(ch * 16, 16), 16)

    def hd_copy(b, d, source, there):
        take = pl.ds(pl.multiple_of(source * 16, 16), 16)
        return remote(
            hidden.at[b, take], hidden.at[b, take], hd_send.at[b, d], hd_recv.at[b, d], {"chan": there}
        )

    def activate(i, carry):
        b = (z - near_first(i) + NZ) % NZ
        total = parts[b, mine, :].astype(F32)
        for d in range(1, CHAN):
            source = lax.rem(ch - d + CHAN, CHAN)
            rs_copy(b, d, ch, source).wait_recv()
            total = total + sums[b, source].astype(F32)
        squares = jnp.sum(total[:, 2 * HIDL :], axis=1, keepdims=True)
        inv = lax.rsqrt(squares / WIDTH + EPS)
        gate = total[:, 0:HIDL] * inv
        up = total[:, HIDL : 2 * HIDL] * inv
        hidden[b, mine, :] = (gate / (1.0 + jnp.exp(-gate)) * up).astype(BF16)
        for d in range(1, CHAN):
            hd_copy(b, d, ch, lax.rem(ch + d, CHAN)).start()
        return carry

    lax.fori_loop(0, NZ, activate, 0)

    def xs_copy(b):
        return remote(x_out.at[b], x_in.at[b], xs_send.at[b], xs_recv.at[b], {"seq": other})

    ours = pl.ds(pl.multiple_of(xh * CAP, CAP), CAP)
    theirs = pl.ds(pl.multiple_of((1 - xh) * CAP, CAP), CAP)

    def contract(i, carry):
        b = (z - near_first(i) + NZ) % NZ
        for d in range(1, CHAN):
            hd_copy(b, d, lax.rem(ch - d + CHAN, CHAN), ch).wait_recv()
        x_out[b] = dot(hidden[b, theirs, :], contract_ref[...]).astype(BF16)
        xs_copy(b).start()
        kept[b] = dot(hidden[b, ours, :], contract_ref[...])
        return carry

    lax.fori_loop(0, NZ, contract, 0)

    def zs_copy(d, b, source):
        return remote(
            z_out.at[b], z_in.at[source], zs_send.at[d], zs_recv.at[d], {"seq": xh * NZ + b}
        )

    def pass_on(i, carry):
        d = near_first(i)
        b = (z + d) % NZ
        xs_copy(b).wait_recv()
        z_out[b] = (kept[b] + x_in[b].astype(F32)).astype(BF16)
        zs_copy(d, b, z).start()
        return carry

    lax.fori_loop(1, NZ, pass_on, 0)
    xs_copy(z).wait_recv()
    out_ref[...] = kept[z] + x_in[z].astype(F32)

    def collect(i, carry):
        d = near_first(i)
        source = (z - d + NZ) % NZ
        zs_copy(d, z, source).wait_recv()
        out_ref[...] += z_in[source].astype(F32)
        return carry

    lax.fori_loop(1, NZ, collect, 0)

    def wait_sends(i, carry):
        fw_copy(i, xh).wait_send()
        xs_copy(i).wait_send()
        for d in range(1, CHAN):
            rs_copy(i, d, ch, ch).wait_send()
            hd_copy(i, d, ch, ch).wait_send()
        return carry

    lax.fori_loop(0, NZ, wait_sends, 0)

    def wait_z_sends(d, carry):
        ag_copy(d, me, other).wait_send()
        zs_copy(d, z, z).wait_send()
        return carry

    lax.fori_loop(1, NZ, wait_z_sends, 0)


def expert_call(*args):
    vm = pl.BlockSpec(memory_space=pltpu.VMEM)
    dma = pltpu.SemaphoreType.DMA
    return pl.pallas_call(
        expert_kernel,
        out_shape=jax.ShapeDtypeStruct((CAP, CH), F32),
        in_specs=[vm] * len(args),
        out_specs=vm,
        scratch_shapes=[
            pltpu.VMEM((SEQ, CAP, CH), BF16),
            pltpu.VMEM((NZ, 128, RSW), BF16),
            pltpu.VMEM((NZ, CHAN, 16, RSW), BF16),
            pltpu.VMEM((NZ, 128, HIDL), BF16),
            pltpu.VMEM((NZ, CAP, CH), BF16),
            pltpu.VMEM((NZ, CAP, CH), BF16),
            pltpu.VMEM((NZ, CAP, CH), F32),
            pltpu.VMEM((NZ, CAP, CH), BF16),
            pltpu.VMEM((NZ, CAP, CH), BF16),
        ]
        + [dma((NZ,))] * 4
        + [dma((NZ, CHAN))] * 4
        + [dma((NZ,))] * 4,
        compiler_params=pltpu.CompilerParams(
            collective_id=1, has_side_effects=True, vmem_limit_bytes=VMEM_LIMIT
        ),
        name="expert",
    )(*args)


def head_kernel(
    mamba_ref, gmap_ref, expert_ref, pick_ref, closing_ref, lexicon_ref, div_ref,
    layer_ref, prob_ref,
    held, acc, squares, chan_stats, seq_stats,
    z_send, z_recv, a_send, a_recv, b_send, b_recv, c_send, c_recv, s_send, s_recv,
):
    me = lax.axis_index("seq")
    ch = lax.axis_index("chan")
    xh, z = me // NZ, me % NZ
    y, xl = ch // 2, ch % 2
    x = xh * 2 + xl
    barrier = pltpu.get_barrier_semaphore()
    greet("seq", SEQ, me)
    greet("chan", CHAN, ch)
    diagonal = {"seq": (1 - xh) * NZ + z, "chan": y * 2 + 1 - xl}
    pl.semaphore_signal(barrier, inc=1, device_id=diagonal, device_id_type=MESH)

    hi, lo = split2(expert_ref[...])
    gmap = gmap_ref[:, 0:CAP]
    layer = (mamba_ref[...].astype(F32) + dot(gmap, hi) + dot(gmap, lo)).astype(BF16)
    layer_ref[...] = layer
    pick = (iota((16, TOK), 1) == pick_ref[...]).astype(F32).astype(BF16)
    picked = dot(pick, layer).astype(BF16)
    own = pl.ds(pl.multiple_of(z * 16, 16), 16)
    held[0, y, x, own, :] = picked[:, 0:512]
    held[1, y, x, own, :] = picked[:, 512:1024]
    pl.semaphore_wait(barrier, 15 + 7 + 1)

    def at_x(there):
        return {"seq": (there // 2) * NZ + z, "chan": y * 2 + there % 2}

    def at_y(there):
        return {"chan": there * 2 + xl}

    def z_copy(d, source, there):
        ref = held.at[:, y, x, pl.ds(pl.multiple_of(source * 16, 16), 16), :]
        return remote(ref, ref, z_send.at[d], z_recv.at[d], {"seq": xh * NZ + there})

    def send_z(i, carry):
        d = near_first(i)
        z_copy(d, z, (z + d) % NZ).start()
        return carry

    lax.fori_loop(1, NZ, send_z, 0)

    def piece(h, yy, xx):
        return held.at[h, yy, xx]

    def first_copy(h, d, yy, xx, there):
        ref = piece(h, yy, xx)
        return remote(ref, ref, a_send.at[h, d], a_recv.at[h, d], there)

    def second_copy(h, k, d, yy, xx, there):
        ref = piece(h, yy, xx)
        return remote(ref, ref, b_send.at[h, k, d], b_recv.at[h, k, d], there)

    def wait_z(d, carry):
        z_copy(d, (z - d + NZ) % NZ, z).wait_recv()
        return carry

    lax.fori_loop(1, NZ, wait_z, 0)
    for d in (1, 3, 2):
        first_copy(0, d, y, x, at_y((y + d) % 4)).start()
        first_copy(1, d, y, x, at_x((x + d) % 4)).start()
    for d in (1, 3, 2):
        second_copy(0, 0, d, y, x, at_x((x + d) % 4)).start()
        second_copy(1, 0, d, y, x, at_y((y + d) % 4)).start()

    acc[...] = jnp.zeros_like(acc)
    squares[...] = jnp.zeros_like(squares)

    def use(h, yy, xx):
        upper, right = xx // 2, xx % 2
        first = pl.multiple_of((yy * 2 + right) * CH + h * 512, 512)
        v = held[h, yy, xx].astype(F32)
        squares[upper] += jnp.sum(v * v, axis=1, keepdims=True)
        scaled = (v * closing_ref[:, pl.ds(first, 512)]).astype(BF16)
        acc[upper] += dot(scaled, lexicon_ref[pl.ds(first, 512), :])

    def own_pieces(h, carry):
        use(h, y, x)
        return carry

    lax.fori_loop(0, 2, own_pieces, 0)
    for d in (1, 3, 2):
        yy, xx = (y - d + 4) % 4, (x - d + 4) % 4
        first_copy(0, d, yy, x, at_y(y)).wait_recv()
        first_copy(1, d, y, xx, at_x(x)).wait_recv()
        for e in (1, 3, 2):
            second_copy(0, d, e, yy, x, at_x((x + e) % 4)).start()
            second_copy(1, d, e, y, xx, at_y((y + e) % 4)).start()
    for d in (1, 3, 2):
        use(0, (y - d + 4) % 4, x)
        use(1, y, (x - d + 4) % 4)
    def last_pieces(k, carry):
        for e in (1, 3, 2):
            yy, xx = (y - k + 4) % 4, (x - e + 4) % 4
            second_copy(0, k, e, yy, xx, at_x(x)).wait_recv()
            use(0, yy, xx)
            yy, xx = (y - e + 4) % 4, (x - k + 4) % 4
            second_copy(1, k, e, yy, xx, at_y(y)).wait_recv()
            use(1, yy, xx)
        return carry

    lax.fori_loop(0, 4, last_pieces, 0)

    inv = lax.rsqrt(squares[...] / WIDTH + EPS).reshape(TOK, 1)
    scores = acc[...].reshape(TOK, TOK) * inv / div_ref[0, 0]
    top = jnp.max(scores, axis=1, keepdims=True)
    mass = jnp.sum(jnp.exp(scores - top), axis=1, keepdims=True)
    chan_stats[ch, 0] = jnp.transpose(jnp.broadcast_to(top, (TOK, 128)))[0:8, :]
    chan_stats[ch, 1] = jnp.transpose(jnp.broadcast_to(mass, (TOK, 128)))[0:8, :]

    def chan_copy(d, source, there):
        ref = chan_stats.at[source]
        return remote(ref, ref, c_send.at[d], c_recv.at[d], {"chan": there})

    def send_c(d, carry):
        chan_copy(d, ch, lax.rem(ch + d, CHAN)).start()
        return carry

    lax.fori_loop(1, CHAN, send_c, 0)

    def wait_c(d, carry):
        chan_copy(d, lax.rem(ch - d + CHAN, CHAN), ch).wait_recv()
        return carry

    lax.fori_loop(1, CHAN, wait_c, 0)

    def join(ref):
        tops = ref[:, 0]
        top = jnp.max(tops, axis=0)
        return top, jnp.sum(ref[:, 1] * jnp.exp(tops - top[None]), axis=0)

    seq_stats[me, 0], seq_stats[me, 1] = join(chan_stats)

    def seq_copy(d, source, there):
        ref = seq_stats.at[source]
        return remote(ref, ref, s_send.at[d], s_recv.at[d], {"seq": there})

    def send_s(d, carry):
        seq_copy(d, me, lax.rem(me + d, SEQ)).start()
        return carry

    lax.fori_loop(1, SEQ, send_s, 0)

    def wait_s(d, carry):
        seq_copy(d, lax.rem(me - d + SEQ, SEQ), me).wait_recv()
        return carry

    lax.fori_loop(1, SEQ, wait_s, 0)
    top, mass = join(seq_stats)
    norm = top + jnp.log(mass)
    column = jnp.transpose(jnp.broadcast_to(norm[0:1, :], (128, TOK)))[:, 0:1]
    prob_ref[...] = scores - column

    def wait_sends(d, carry):
        z_copy(d, z, z).wait_send()
        chan_copy(d, ch, ch).wait_send()
        return carry

    lax.fori_loop(1, NZ, wait_sends, 0)

    def wait_s_sends(d, carry):
        seq_copy(d, me, me).wait_send()
        return carry

    lax.fori_loop(1, SEQ, wait_s_sends, 0)

    def wait_a_sends(d, carry):
        for h in range(2):
            first_copy(h, d, y, x, at_y(y)).wait_send()
            for k in range(4):
                second_copy(h, k, d, y, x, at_y(y)).wait_send()
        return carry

    lax.fori_loop(1, 4, wait_a_sends, 0)


def head_call(*args):
    vm = pl.BlockSpec(memory_space=pltpu.VMEM)
    dma = pltpu.SemaphoreType.DMA
    return pl.pallas_call(
        head_kernel,
        out_shape=(
            jax.ShapeDtypeStruct((TOK, CH), BF16),
            jax.ShapeDtypeStruct((TOK, TOK), F32),
        ),
        in_specs=[vm] * (len(args) - 1) + [pl.BlockSpec(memory_space=pltpu.SMEM)],
        out_specs=(vm, vm),
        scratch_shapes=[
            pltpu.VMEM((2, 4, 4, 128, 512), BF16),
            pltpu.VMEM((2, 128, TOK), F32),
            pltpu.VMEM((2, 128, 1), F32),
            pltpu.VMEM((CHAN, 2, 8, TOK), F32),
            pltpu.VMEM((SEQ, 2, 8, TOK), F32),
            dma((NZ,)), dma((NZ,)),
            dma((2, 4)), dma((2, 4)),
            dma((2, 4, 4)), dma((2, 4, 4)),
            dma((CHAN,)), dma((CHAN,)),
            dma((SEQ,)), dma((SEQ,)),
        ],
        compiler_params=pltpu.CompilerParams(
            collective_id=2, has_side_effects=True, vmem_limit_bytes=VMEM_LIMIT
        ),
        name="head",
    )(*args)


def shards(
    recurrence_feed,
    memory_write_matrix,
    memory_read_matrix,
    log_shrink_table,
    skip_connection_scale,
    specialist_choices,
    specialist_mixing_shares,
    specialist_rescale_vector,
    specialist_switch_matrix,
    specialist_widen_matrix,
    specialist_contract_matrix,
    closing_rescale_vector,
    lexicon_matrix,
    softness_divisor,
    picked_entry_offsets,
):
    mamba, slots, gmap = scan_call(
        recurrence_feed,
        memory_write_matrix,
        memory_read_matrix,
        log_shrink_table,
        skip_connection_scale.reshape(1, -1),
        specialist_choices,
        specialist_mixing_shares,
    )
    expert = expert_call(
        slots,
        specialist_rescale_vector.reshape(1, -1),
        specialist_switch_matrix,
        specialist_widen_matrix,
        specialist_contract_matrix,
    )
    return head_call(
        mamba,
        gmap,
        expert,
        picked_entry_offsets.reshape(-1, 1),
        closing_rescale_vector.reshape(1, -1),
        lexicon_matrix,
        softness_divisor.reshape(1, 1),
    )


def solution(mesh):
    in_specs = (
        P(("dp", "seq"), "chan"),
        P(("dp", "seq"), None),
        P(("dp", "seq"), None),
        P(("dp", "seq"), "chan"),
        P("chan"),
        P(("dp", "seq"), None),
        P(("dp", "seq"), None),
        P("chan"),
        P("chan", "seq"),
        P("chan", "seq"),
        P("seq", "chan"),
        P(),
        P(None, ("seq", "chan")),
        P(),
        P(("dp", "seq")),
    )
    out_specs = (P(("dp", "seq"), "chan"), P("dp", ("seq", "chan")))
    return jax.shard_map(shards, mesh=mesh, in_specs=in_specs, out_specs=out_specs, check_vma=False)
```

time: 1480 us -> 219 us (0.15)
  blocking collectives: 771 us -> 0 us
  waiting for transfers between devices: 627 us -> 0 us
  Pallas kernels: 0 us -> 208 us
  other arithmetic: 28 us -> 0 us
  matrix products: 23.2 us -> 0 us
    all_gather x4 -> x0, blocking collectives: 754 us -> none  [the longest x2 682 us: joined(): gathered = jax.tree.map(lambda a: lax.all_gather(a, axis), part)]
    all_gather x3 -> x0, waiting for transfers between devices: 274 us -> none  [the longest x1 97.2 us: shards(): lax.all_gather(normed_rows, 'seq', axis=0, tiled=True)]
    pallas_call x0 -> x3, Pallas kernels: none -> 208 us  [the longest x1 121 us: expert_call(): pl.pallas_call(expert_kernel, out_shape=jax.ShapeDtypeStruct((CAP, CH), F...]
    reduce_scatter x1 -> x0, waiting for transfers between devices: 208 us -> none  [shards(): lax.psum_scatter(expert_out.astype(jnp.bfloat16), 'seq', scatter_dimensio...]
    psum x1 -> x0, waiting for transfers between devices: 146 us -> none  [shards(): lax.psum(up_part.astype(jnp.bfloat16), 'chan').astype(jnp.float32)]
    dot_general x9 -> x0, matrix products: 23.2 us -> none  [the longest x1 5.28 us: shards(): jnp.dot(hidden, specialist_contract_matrix, preferred_element_type=jnp.fl...]
    select_n x20 -> x0, other arithmetic: 18.9 us -> none  [the longest x16 18.8 us: hop(): return jax.tree.map(lambda a, b: jnp.where(reached, a, b), new, before)]
    psum x1 -> x0, blocking collectives: 17.6 us -> none  [shards(): total_squares = lax.psum(jnp.sum(values * values, axis=-1), 'chan')]
  transfers between devices with their start and end apart: 5 -> 0, of which waited for: 5 -> 0; matrix products, arithmetic and copies ran while one was open for 0% -> 0% of each run, Pallas kernels for 0% -> 0%
where the time goes in v1:
time: 219 us
  Pallas kernels  208 us (95%)
  local copies, waits for them, and re-layouts  9.24 us (4%)
    pallas_call x1, Pallas kernels, expert_call(): pl.pallas_call(expert_kernel, out_shape=jax.ShapeDtypeStruct((CAP, CH), F...  121 us
    pallas_call x1, Pallas kernels, head_call(): pl.pallas_call(head_kernel, out_shape=(jax.ShapeDtypeStruct((TOK, CH), BF...  56.3 us
    pallas_call x1, Pallas kernels, scan_call(): pl.pallas_call(scan_kernel, out_shape=(jax.ShapeDtypeStruct((TOK, CH), BF...  31.2 us
    unnamed x5, local copies, waits for them, and re-layouts  7.91 us

profile of v1, /device:TPU:2, one launch (start us, length us, event | category | flops | bytes accessed | tf_op | source)
XLA Modules:
  0.0 218.7 jit_solution(13595957542912248628)
XLA Ops:
  1.3 1.3 copy.20.pick_ref
  2.6 1.4 copy.19.share_ref
  4.0 1.5 copy.17.la_ref
  5.5 1.5 copy.18.choice_ref
  7.0 31.2 %scan.1 = (bf16[256,1024]{1,0:T(8,128)(2,1)}, bf16[64,1024]{1,0:T(8,128)(2,1)}, bf16[256,128]{1,0:T(8,128)(2,1)}) custom-call(bf16[256,1024]{1,0:T(8,128)(2,1)} %x_ref.1, bf16[256,128]{1,0:T(8,128)(2,1)} %b_ref.1, bf16[256,128]{1,0:T(8,128)(2,1)} %c_ref.1, f32[256,16]{1,0:T(8,128)} %copy.17.la_ref, f32[1,16]{1,0:T(1,128)} %bitcast.8, ...), custom_call_target="tpu_custom_call" | custom-call | tf_op jit(solution)/shard_map/scan/pallas_call | solution.py:217
  38.1 120.7 %expert.1.expert_ref = f32[64,1024]{1,0:T(8,128)} custom-call(bf16[64,1024]{1,0:T(8,128)(2,1)} %get-tuple-element.7.slots_ref, f32[1,1024]{1,0:T(1,128)} %bitcast.7, bf16[1024,768]{1,0:T(8,128)(2,1)} %switch_ref.1, bf16[1024,768]{1,0:T(8,128)(2,1)} %widen_ref.1, bf16[768,1024]{1,0:T(8,128)(2,1)} %contract_ref.1), custom_call_target="tpu_custom_call" | custom-call | tf_op jit(solution)/shard_map/expert/pallas_call | solution.py:416
  158.9 56.3 %head.1 = (bf16[256,1024]{1,0:T(8,128)(2,1)}, f32[256,256]{1,0:T(8,128)}) custom-call(bf16[256,1024]{1,0:T(8,128)(2,1)} %get-tuple-element.5.mamba_ref, bf16[256,128]{1,0:T(8,128)(2,1)} %get-tuple-element.6.gmap_ref, f32[64,1024]{1,0:T(8,128)} %expert.1.expert_ref, s32[16,1]{1,0:T(8,128)} %copy.20.pick_ref, f32[1,8192]{1,0:T(1,128)} %bitcast.6, ...), custom_call_target="tpu_custom_call" | custom-call | tf_op jit(solution)/shard_map/head/pallas_call | solution.py:624
  215.1 1.9 copy.24
  217.0 1.7 copy.25

commit v2 on v1

--- a/solution.py
+++ b/solution.py
@@ -15,7 +15,6 @@
 NZ = 8
 CAP = 64
 HIDL = 768
-RSW = 2 * HIDL + 128
 WIDTH = 8192
 EPS = 1e-5
 VMEM_LIMIT = 56 * 1024 * 1024
@@ -74,12 +73,12 @@
     greet("seq", SEQ, me)
 
     wide[...] = jnp.zeros_like(wide)
-    wide[0:TOK, 0:16] = la_ref[...]
-    wide[TOK : TOK + 1, 0:16] = skip_ref[...]
+    wide[0:16, :] = la_ref[...]
     tril = (iota((TOK, TOK), 0) >= iota((TOK, TOK), 1)).astype(F32)
-    tril_bf = tril.astype(BF16)
-    hi, mid, lo = split3(wide[0:TOK, :])
-    cum = dot(tril_bf, hi) + dot(tril_bf, mid) + dot(tril_bf, lo)
+    triu_bf = (iota((TOK, TOK), 0) <= iota((TOK, TOK), 1)).astype(F32).astype(BF16)
+    hi, mid, lo = split3(wide[...])
+    cum_t = dot(hi, triu_bf) + dot(mid, triu_bf) + dot(lo, triu_bf)
+    cum = jnp.transpose(cum_t)
     last = cum[TOK - 1 : TOK, :]
     spread_map = (iota((128, CH), 1) // 64 == iota((128, CH), 0)).astype(F32).astype(BF16)
 
@@ -125,7 +124,6 @@
         c_ref[...], b_ref[...], (((1,), (1,)), ((), ())), preferred_element_type=F32
     )
     scores = scores * tril
-    cum_t = jnp.transpose(cum)
     lane = iota((128, 128), 1)
 
     def heads(pairs):
@@ -175,18 +173,19 @@
 
     heads(range(4, 8))
 
-    first, second = choice_ref[:, 0:1] == 0, choice_ref[:, 1:2] == 0
+    first, second = choice_ref[0:1, :] == 0, choice_ref[1:2, :] == 0
     used = jnp.where(first, 1.0, 0.0) + jnp.where(second, 1.0, 0.0)
-    gate = jnp.where(first, share_ref[:, 0:1].astype(F32), 0.0) + jnp.where(
-        second, share_ref[:, 1:2].astype(F32), 0.0
+    gate = jnp.where(first, share_ref[0:1, :].astype(F32), 0.0) + jnp.where(
+        second, share_ref[1:2, :].astype(F32), 0.0
     )
-    used = jnp.broadcast_to(used, (TOK, 128))
-    place = dot(tril_bf, used.astype(BF16)) - 1.0
-    slot_map = jnp.where(place == iota((TOK, 128), 1).astype(F32), used, 0.0)
-    gmap_ref[...] = (slot_map * gate).astype(BF16)
-    slot_t = jnp.transpose(slot_map)[0:CAP, :].astype(BF16)
-
-    skip_wide = expand(wide[TOK : TOK + 8, :])[0:1, :]
+    used = jnp.broadcast_to(used, (128, TOK))
+    place = dot(used.astype(BF16), triu_bf) - 1.0
+    slot_map = jnp.where(place == iota((128, TOK), 0).astype(F32), used, 0.0)
+    gmap_ref[...] = jnp.transpose(slot_map * gate).astype(BF16)
+    slot_t = slot_map[0:CAP, :].astype(BF16)
+
+    skip = jnp.concatenate([skip_ref[...], jnp.zeros((1, 112), F32)], axis=1)
+    skip_wide = expand(jnp.broadcast_to(skip, (8, 128)))[0:1, :]
     cum_wide = expand(jnp.exp(cum))
 
     def wait_p(d, carry):
@@ -224,7 +223,7 @@
         in_specs=[vm] * len(args),
         out_specs=(vm, vm, vm),
         scratch_shapes=[
-            pltpu.VMEM((TOK + 8, 128), F32),
+            pltpu.VMEM((128, TOK), F32),
             pltpu.VMEM((128, CH), BF16),
             pltpu.VMEM((SEQ, 16, 512), BF16),
             pltpu.VMEM((SEQ, 8, 128), F32),
@@ -248,166 +247,243 @@
 def expert_kernel(
     slots_ref, rescale_ref, switch_ref, widen_ref, contract_ref,
     out_ref,
-    rows, parts, sums, hidden, x_out, x_in, kept, z_out, z_in,
-    ag_send, ag_recv, fw_send, fw_recv, rs_send, rs_recv, hd_send, hd_recv,
+    rows, pg, pu, g1, u1, us, g2, u2, hidden, x_out, x_in, kept, z_out, z_in,
+    ag_send, ag_recv, fw_send, fw_recv,
+    g1_send, g1_recv, u1_send, u1_recv, g2_send, g2_recv, u2_send, u2_recv,
+    hx_send, hx_recv, hy_send, hy_recv,
     xs_send, xs_recv, zs_send, zs_recv,
 ):
     me = lax.axis_index("seq")
     ch = lax.axis_index("chan")
     xh, z = me // NZ, me % NZ
-    other = (1 - xh) * NZ + z
+    y, xl = ch // 2, ch % 2
+    other = {"seq": (1 - xh) * NZ + z}
+    beside = {"chan": y * 2 + 1 - xl}
     barrier = pltpu.get_barrier_semaphore()
 
-    def greet_z(d, carry):
-        pl.semaphore_signal(
-            barrier, inc=1, device_id={"seq": xh * NZ + (z + d) % NZ}, device_id_type=MESH
+    def at_z(there):
+        return {"seq": xh * NZ + there % NZ}
+
+    def at_y(there):
+        return {"chan": (there % 4) * 2 + xl}
+
+    for d in range(1, NZ):
+        pl.semaphore_signal(barrier, inc=1, device_id=at_z(z + d), device_id_type=MESH)
+    for d in range(1, 4):
+        pl.semaphore_signal(barrier, inc=1, device_id=at_y(y + d), device_id_type=MESH)
+    pl.semaphore_signal(barrier, inc=1, device_id=other, device_id_type=MESH)
+    pl.semaphore_signal(barrier, inc=1, device_id=beside, device_id_type=MESH)
+    rows[me] = slots_ref[...]
+    pl.semaphore_wait(barrier, 7 + 3 + 1 + 1)
+
+    def order(i):
+        return (z - near_first(i) + NZ) % NZ
+
+    def sixteen(start):
+        return pl.ds(pl.multiple_of(start, 16), 16)
+
+    fw = remote(rows.at[me], rows.at[me], fw_send, fw_recv, other)
+
+    def ag_copy(way, k, half, block):
+        row = half * NZ + block % NZ
+        ref = rows.at[row]
+        there = at_z(z + 1 if way == 0 else z + NZ - 1)
+        return remote(ref, ref, ag_send.at[way, k, half], ag_recv.at[way, k, half], there)
+
+    def ag_last(way, half, block):
+        ref = rows.at[half * NZ + block % NZ, pl.ds(32 * way, 32)]
+        there = at_z(z + 1 if way == 0 else z + NZ - 1)
+        return remote(ref, ref, ag_send.at[way, 4, half], ag_recv.at[way, 4, half], there)
+
+    def behind(way, k):
+        return z - k + NZ if way == 0 else z + k
+
+    fw.start()
+    for way in range(2):
+        ag_copy(way, 1, xh, z).start()
+
+    def gather(i):
+        @pl.when(i == 0)
+        def _():
+            remote(rows.at[(1 - xh) * NZ + z], rows.at[(1 - xh) * NZ + z], fw_send, fw_recv, other).wait_recv()
+            for way in range(2):
+                ag_copy(way, 1, 1 - xh, z).start()
+
+        @pl.when((i % 2 == 1) & (i < NZ - 1))
+        def _():
+            k = (i + 1) // 2
+            for j in range(2):
+                half = xh + j - 2 * j * xh
+                for way in range(2):
+                    ag_copy(way, k, half, behind(way, k)).wait_recv()
+
+                    @pl.when(k < 3)
+                    def _():
+                        ag_copy(way, k + 1, half, behind(way, k)).start()
+
+                    @pl.when(k == 3)
+                    def _():
+                        ag_last(way, half, behind(way, k)).start()
+
+        @pl.when(i == NZ - 1)
+        def _():
+            for way in range(2):
+                for half in range(2):
+                    ag_last(way, half, z + 4).wait_recv()
+
+    def g1_copy(b):
+        return remote(pg.at[b, 1 - xl], g1.at[b], g1_send.at[b], g1_recv.at[b], beside)
+
+    def u1_copy(b, d, there, source):
+        return remote(
+            pu.at[b, :, sixteen(there * 16)], u1.at[b, source], u1_send.at[b, d], u1_recv.at[b, d], at_y(there)
         )
-        return carry
-
-    lax.fori_loop(1, NZ, greet_z, 0)
-    pl.semaphore_signal(barrier, inc=1, device_id={"seq": other}, device_id_type=MESH)
-    greet("chan", CHAN, ch)
-    rows[me] = slots_ref[...]
-    pl.semaphore_wait(barrier, 7 + 1 + 7)
-
-    def ag_copy(d, src, there):
-        return remote(rows.at[src], rows.at[src], ag_send.at[d], ag_recv.at[d], {"seq": there})
-
-    def fw_copy(b, half):
-        src = half * NZ + b
-        return remote(rows.at[src], rows.at[src], fw_send.at[b], fw_recv.at[b], {"seq": other})
-
-    fw_copy(z, xh).start()
-
-    def send_ag(i, carry):
-        d = near_first(i)
-        ag_copy(d, me, xh * NZ + (z + d) % NZ).start()
-        return carry
-
-    lax.fori_loop(1, NZ, send_ag, 0)
-
-    def forward(i):
-        d = near_first(i)
-        b = (z - d + NZ) % NZ
-        ag_copy(d, xh * NZ + b, other).wait_recv()
-        fw_copy(b, xh).start()
-
-    def rs_copy(b, d, there, source):
-        take = pl.ds(pl.multiple_of(there * 16, 16), 16)
+
+    def g2_copy(b, d, there, source):
         return remote(
-            parts.at[b, take], sums.at[b, source], rs_send.at[b, d], rs_recv.at[b, d], {"chan": there}
+            pg.at[b, xl, sixteen(there * 16)], g2.at[b, source], g2_send.at[b, d], g2_recv.at[b, d], at_y(there)
         )
 
-    def project(i, carry):
-        @pl.when(i < NZ - 1)
-        def _():
-            forward(i + 1)
-
-        b = (z - near_first(i) + NZ) % NZ
-        fw_copy(b, 1 - xh).wait_recv()
+    def u2_copy(b):
+        return remote(us.at[b, 1 - xl], u2.at[b], u2_send.at[b], u2_recv.at[b], beside)
+
+    lane = iota((128, 128), 1)
+
+    def project(i):
+        gather(i)
+        b = order(i)
         v = jnp.concatenate([rows[b], rows[NZ + b]], axis=0).astype(F32)
         squares = jnp.sum(v * v, axis=1, keepdims=True)
         scaled = (v * rescale_ref[...]).astype(BF16)
-        parts[b, :, 0:HIDL] = dot(scaled, switch_ref[...]).astype(BF16)
-        parts[b, :, HIDL : 2 * HIDL] = dot(scaled, widen_ref[...]).astype(BF16)
         hi, mid, lo = split3(squares)
-        lane = iota((128, 128), 1)
-        parts[b, :, 2 * HIDL :] = jnp.where(
+        extra = jnp.where(
             lane == 0,
             hi.astype(F32),
             jnp.where(lane == 1, mid.astype(F32), jnp.where(lane == 2, lo.astype(F32), 0.0)),
         ).astype(BF16)
-        for d in range(1, CHAN):
-            rs_copy(b, d, lax.rem(ch + d, CHAN), ch).start()
-        return carry
-
-    lax.fori_loop(0, NZ, project, 0)
-
-    mine = pl.ds(pl.multiple_of(ch * 16, 16), 16)
-
-    def hd_copy(b, d, source, there):
-        take = pl.ds(pl.multiple_of(source * 16, 16), 16)
-        return remote(
-            hidden.at[b, take], hidden.at[b, take], hd_send.at[b, d], hd_recv.at[b, d], {"chan": there}
-        )
-
-    def activate(i, carry):
-        b = (z - near_first(i) + NZ) % NZ
-        total = parts[b, mine, :].astype(F32)
-        for d in range(1, CHAN):
-            source = lax.rem(ch - d + CHAN, CHAN)
-            rs_copy(b, d, ch, source).wait_recv()
-            total = total + sums[b, source].astype(F32)
-        squares = jnp.sum(total[:, 2 * HIDL :], axis=1, keepdims=True)
+        pg[b, :, :, HIDL:] = extra.reshape(2, 64, 128)
+        pg[b, :, :, 0:HIDL] = dot(scaled, switch_ref[...]).astype(BF16).reshape(2, 64, HIDL)
+        g1_copy(b).start()
+        pu[b] = dot(scaled, widen_ref[...]).astype(BF16).reshape(2, 64, HIDL)
+        for d in (1, 3, 2):
+            u1_copy(b, d, (y + d) % 4, y).start()
+
+    def fold(i):
+        b = order(i)
+        g1_copy(b).wait_recv()
+        pg[b, xl] = (pg[b, xl].astype(F32) + g1[b].astype(F32)).astype(BF16)
+        for d in (1, 3, 2):
+            g2_copy(b, d, (y + d) % 4, y).start()
+        total = pu[b, :, sixteen(y * 16), :].astype(F32)
+        for d in (1, 3, 2):
+            source = (y - d + 4) % 4
+            u1_copy(b, d, y, source).wait_recv()
+            total = total + u1[b, source].astype(F32)
+        us[b] = total.astype(BF16)
+        u2_copy(b).start()
+
+    def hx_copy(b, owner):
+        ref = hidden.at[b, owner, sixteen(y * 16)]
+        return remote(ref, ref, hx_send.at[b], hx_recv.at[b], beside)
+
+    def hy_copy(b, owner, d, source, there):
+        ref = hidden.at[b, owner, sixteen(source * 16)]
+        return remote(ref, ref, hy_send.at[b, owner, d], hy_recv.at[b, owner, d], at_y(there))
+
+    def activate(i):
+        b = order(i)
+        gate = pg[b, xl, sixteen(y * 16), :].astype(F32)
+        for d in (1, 3, 2):
+            source = (y - d + 4) % 4
+            g2_copy(b, d, y, source).wait_recv()
+            gate = gate + g2[b, source].astype(F32)
+        u2_copy(b).wait_recv()
+        up = us[b, xl].astype(F32) + u2[b].astype(F32)
+        squares = jnp.sum(gate[:, HIDL:], axis=1, keepdims=True)
         inv = lax.rsqrt(squares / WIDTH + EPS)
-        gate = total[:, 0:HIDL] * inv
-        up = total[:, HIDL : 2 * HIDL] * inv
-        hidden[b, mine, :] = (gate / (1.0 + jnp.exp(-gate)) * up).astype(BF16)
-        for d in range(1, CHAN):
-            hd_copy(b, d, ch, lax.rem(ch + d, CHAN)).start()
-        return carry
-
-    lax.fori_loop(0, NZ, activate, 0)
+        gate = gate[:, 0:HIDL] * inv
+        hidden[b, xl, sixteen(y * 16), :] = (gate / (1.0 + jnp.exp(-gate)) * (up * inv)).astype(BF16)
+        hx_copy(b, xl).start()
+        for d in (1, 3, 2):
+            hy_copy(b, xl, d, y, y + d).start()
+
+    def relay(i):
+        b = order(i)
+        hx_copy(b, 1 - xl).wait_recv()
+        for d in (1, 3, 2):
+            hy_copy(b, 1 - xl, d, y, y + d).start()
 
     def xs_copy(b):
-        return remote(x_out.at[b], x_in.at[b], xs_send.at[b], xs_recv.at[b], {"seq": other})
-
-    ours = pl.ds(pl.multiple_of(xh * CAP, CAP), CAP)
-    theirs = pl.ds(pl.multiple_of((1 - xh) * CAP, CAP), CAP)
-
-    def contract(i, carry):
-        b = (z - near_first(i) + NZ) % NZ
-        for d in range(1, CHAN):
-            hd_copy(b, d, lax.rem(ch - d + CHAN, CHAN), ch).wait_recv()
-        x_out[b] = dot(hidden[b, theirs, :], contract_ref[...]).astype(BF16)
+        return remote(x_out.at[b], x_in.at[b], xs_send.at[b], xs_recv.at[b], other)
+
+    def contract(i):
+        b = order(i)
+        for half in range(2):
+            for d in (1, 3, 2):
+                hy_copy(b, half, d, (y - d + 4) % 4, y).wait_recv()
+        x_out[b] = dot(hidden[b, 1 - xh], contract_ref[...]).astype(BF16)
         xs_copy(b).start()
-        kept[b] = dot(hidden[b, ours, :], contract_ref[...])
-        return carry
-
-    lax.fori_loop(0, NZ, contract, 0)
-
-    def zs_copy(d, b, source):
-        return remote(
-            z_out.at[b], z_in.at[source], zs_send.at[d], zs_recv.at[d], {"seq": xh * NZ + b}
-        )
-
-    def pass_on(i, carry):
-        d = near_first(i)
-        b = (z + d) % NZ
+        kept[b] = dot(hidden[b, xh], contract_ref[...])
+
+    def zs_copy(i, b, source):
+        return remote(z_out.at[b], z_in.at[source], zs_send.at[i], zs_recv.at[i], at_z(b))
+
+    def pass_on(i):
+        b = order(i)
         xs_copy(b).wait_recv()
         z_out[b] = (kept[b] + x_in[b].astype(F32)).astype(BF16)
-        zs_copy(d, b, z).start()
-        return carry
-
-    lax.fori_loop(1, NZ, pass_on, 0)
-    xs_copy(z).wait_recv()
+
+        @pl.when(i > 0)
+        def _():
+            zs_copy(i, b, z).start()
+
+    stages = ((project, 0), (fold, 1), (activate, 2), (relay, 3), (contract, 4), (pass_on, 5))
+
+    def step(i, carry):
+        for stage, off in stages:
+
+            @pl.when((i >= off) & (i < off + NZ))
+            def _():
+                stage(i - off)
+
+        return carry
+
+    lax.fori_loop(0, NZ + stages[-1][1], step, 0)
     out_ref[...] = kept[z] + x_in[z].astype(F32)
 
     def collect(i, carry):
-        d = near_first(i)
-        source = (z - d + NZ) % NZ
-        zs_copy(d, z, source).wait_recv()
+        source = (z + near_first(i)) % NZ
+        zs_copy(i, z, source).wait_recv()
         out_ref[...] += z_in[source].astype(F32)
         return carry
 
     lax.fori_loop(1, NZ, collect, 0)
 
-    def wait_sends(i, carry):
-        fw_copy(i, xh).wait_send()
-        xs_copy(i).wait_send()
-        for d in range(1, CHAN):
-            rs_copy(i, d, ch, ch).wait_send()
-            hd_copy(i, d, ch, ch).wait_send()
+    def wait_sends(b, carry):
+        g1_copy(b).wait_send()
+        u2_copy(b).wait_send()
+        hx_copy(b, xl).wait_send()
+        xs_copy(b).wait_send()
+        for d in range(1, 4):
+            u1_copy(b, d, y, y).wait_send()
+            g2_copy(b, d, y, y).wait_send()
+            for half in range(2):
+                hy_copy(b, half, d, y, y).wait_send()
         return carry
 
     lax.fori_loop(0, NZ, wait_sends, 0)
 
-    def wait_z_sends(d, carry):
-        ag_copy(d, me, other).wait_send()
-        zs_copy(d, z, z).wait_send()
+    def wait_z_sends(i, carry):
+        zs_copy(i, z, z).wait_send()
         return carry
 
     lax.fori_loop(1, NZ, wait_z_sends, 0)
+    fw.wait_send()
+    for way in range(2):
+        for half in range(2):
+            ag_last(way, half, z).wait_send()
+            for k in range(1, 4):
+                ag_copy(way, k, half, z).wait_send()
 
 
 def expert_call(*args):
@@ -420,18 +496,25 @@
         out_specs=vm,
         scratch_shapes=[
             pltpu.VMEM((SEQ, CAP, CH), BF16),
-            pltpu.VMEM((NZ, 128, RSW), BF16),
-            pltpu.VMEM((NZ, CHAN, 16, RSW), BF16),
-            pltpu.VMEM((NZ, 128, HIDL), BF16),
+            pltpu.VMEM((NZ, 2, 64, HIDL + 128), BF16),
+            pltpu.VMEM((NZ, 2, 64, HIDL), BF16),
+            pltpu.VMEM((NZ, 64, HIDL + 128), BF16),
+            pltpu.VMEM((NZ, 4, 2, 16, HIDL), BF16),
+            pltpu.VMEM((NZ, 2, 16, HIDL), BF16),
+            pltpu.VMEM((NZ, 4, 16, HIDL + 128), BF16),
+            pltpu.VMEM((NZ, 16, HIDL), BF16),
+            pltpu.VMEM((NZ, 2, 64, HIDL), BF16),
             pltpu.VMEM((NZ, CAP, CH), BF16),
             pltpu.VMEM((NZ, CAP, CH), BF16),
             pltpu.VMEM((NZ, CAP, CH), F32),
             pltpu.VMEM((NZ, CAP, CH), BF16),
             pltpu.VMEM((NZ, CAP, CH), BF16),
-        ]
-        + [dma((NZ,))] * 4
-        + [dma((NZ, CHAN))] * 4
-        + [dma((NZ,))] * 4,
+            dma((2, 5, 2)), dma((2, 5, 2)), dma, dma,
+            dma((NZ,)), dma((NZ,)), dma((NZ, 4)), dma((NZ, 4)),
+            dma((NZ, 4)), dma((NZ, 4)), dma((NZ,)), dma((NZ,)),
+            dma((NZ,)), dma((NZ,)), dma((NZ, 2, 4)), dma((NZ, 2, 4)),
+            dma((NZ,)), dma((NZ,)), dma((NZ,)), dma((NZ,)),
+        ],
         compiler_params=pltpu.CompilerParams(
             collective_id=1, has_side_effects=True, vmem_limit_bytes=VMEM_LIMIT
         ),
@@ -460,7 +543,11 @@
     gmap = gmap_ref[:, 0:CAP]
     layer = (mamba_ref[...].astype(F32) + dot(gmap, hi) + dot(gmap, lo)).astype(BF16)
     layer_ref[...] = layer
-    pick = (iota((16, TOK), 1) == pick_ref[...]).astype(F32).astype(BF16)
+    offsets = jnp.concatenate(
+        [pick_ref[...].astype(F32), jnp.full((1, 112), -1.0, F32)], axis=1
+    )
+    offsets = jnp.transpose(jnp.broadcast_to(offsets, (128, 128)))[0:16, 0:1]
+    pick = (iota((16, TOK), 1).astype(F32) == offsets).astype(F32).astype(BF16)
     picked = dot(pick, layer).astype(BF16)
     own = pl.ds(pl.multiple_of(z * 16, 16), 16)
     held[0, y, x, own, :] = picked[:, 0:512]
@@ -669,10 +756,10 @@
         recurrence_feed,
         memory_write_matrix,
         memory_read_matrix,
-        log_shrink_table,
+        log_shrink_table.T,
         skip_connection_scale.reshape(1, -1),
-        specialist_choices,
-        specialist_mixing_shares,
+        specialist_choices.T,
+        specialist_mixing_shares.T,
     )
     expert = expert_call(
         slots,
@@ -685,7 +772,7 @@
         mamba,
         gmap,
         expert,
-        picked_entry_offsets.reshape(-1, 1),
+        picked_entry_offsets.reshape(1, -1),
         closing_rescale_vector.reshape(1, -1),
         lexicon_matrix,
         softness_divisor.reshape(1, 1),

time: 219 us -> 181 us (0.83)
  Pallas kernels: 208 us -> 175 us
  local copies, waits for them, and re-layouts: 9.24 us -> 3.54 us
    pallas_call x1, Pallas kernels: 121 us -> 86.3 us  [expert_call(): pl.pallas_call(expert_kernel, out_shape=jax.ShapeDtypeStruct((CAP, CH), F...]
    unnamed x5 -> x2, local copies, waits for them, and re-layouts: 7.91 us -> 3.54 us
where the time goes in v2:
time: 181 us; the launch traced here: 180 us
  Pallas kernels  175 us (97%)
  local copies, waits for them, and re-layouts  3.54 us (2%)
    pallas_call x1, Pallas kernels, expert_call(): pl.pallas_call(expert_kernel, out_shape=jax.ShapeDtypeStruct((CAP, CH), F...  86.3 us
    pallas_call x1, Pallas kernels, head_call(): pl.pallas_call(head_kernel, out_shape=(jax.ShapeDtypeStruct((TOK, CH), BF...  57.8 us
    pallas_call x1, Pallas kernels, scan_call(): pl.pallas_call(scan_kernel, out_shape=(jax.ShapeDtypeStruct((TOK, CH), BF...  31.3 us

profile of v2, /device:TPU:2, one launch (start us, length us, event | category | flops | bytes accessed | tf_op | source)
XLA Modules:
  0.0 180.3 jit_solution(9633453405236646585)
XLA Ops:
  1.3 31.3 %scan.1 = (bf16[256,1024]{1,0:T(8,128)(2,1)}, bf16[64,1024]{1,0:T(8,128)(2,1)}, bf16[256,128]{1,0:T(8,128)(2,1)}) custom-call(bf16[256,1024]{1,0:T(8,128)(2,1)} %x_ref.1, bf16[256,128]{1,0:T(8,128)(2,1)} %b_ref.1, bf16[256,128]{1,0:T(8,128)(2,1)} %c_ref.1, f32[16,256]{1,0:T(8,128)} %bitcast.10, f32[1,16]{1,0:T(1,128)} %bitcast.14, s32[2,256]{1,0:T(2,128)} %bitcast.12, ...), custom_call_target="tpu_custom_call" | custom-call | tf_op jit(solution)/shard_map/scan/pallas_call | solution.py:216
  32.6 86.3 %expert.1.expert_ref = f32[64,1024]{1,0:T(8,128)} custom-call(bf16[64,1024]{1,0:T(8,128)(2,1)} %get-tuple-element.7.slots_ref, f32[1,1024]{1,0:T(1,128)} %bitcast.11, bf16[1024,768]{1,0:T(8,128)(2,1)} %switch_ref.1, bf16[1024,768]{1,0:T(8,128)(2,1)} %widen_ref.1, bf16[768,1024]{1,0:T(8,128)(2,1)} %contract_ref.1), custom_call_target="tpu_custom_call" | custom-call | tf_op jit(solution)/shard_map/expert/pallas_call | solution.py:492
  118.9 57.8 %head.1 = (bf16[256,1024]{1,0:T(8,128)(2,1)}, f32[256,256]{1,0:T(8,128)}) custom-call(bf16[256,1024]{1,0:T(8,128)(2,1)} %get-tuple-element.5.mamba_ref, bf16[256,128]{1,0:T(8,128)(2,1)} %get-tuple-element.6.gmap_ref, f32[64,1024]{1,0:T(8,128)} %expert.1.expert_ref, s32[1,16]{1,0:T(1,128)} %bitcast.15, f32[1,8192]{1,0:T(1,128)} %bitcast.9, ...), custom_call_target="tpu_custom_call" | custom-call | tf_op jit(solution)/shard_map/head/pallas_call | solution.py:711
  176.7 1.9 %copy.20 = bf16[256,1024]{1,0:T(8,128)(2,1)} copy(bf16[256,1024]{1,0:T(8,128)(2,1)} %get-tuple-element.10) | data formatting | bytes 1048576
  178.6 1.7 copy.21

commit v3 on v2

--- a/solution.py
+++ b/solution.py
@@ -63,14 +63,13 @@
     lax.fori_loop(1, size, one, 0)
 
 
-def scan_kernel(
+def scan_part(
     x_ref, b_ref, c_ref, la_ref, skip_ref, choice_ref, share_ref,
-    mamba_ref, slots_ref, gmap_ref,
+    mamba_ref, rows, gmap_ref,
     wide, local, taken, decays, prefixes, entry, y_ref,
     dec_send, dec_recv, a_send, a_recv, p_send, p_recv,
 ):
     me = lax.axis_index("seq")
-    greet("seq", SEQ, me)
 
     wide[...] = jnp.zeros_like(wide)
     wide[0:16, :] = la_ref[...]
@@ -87,7 +86,7 @@
         return dot(hi, spread_map) + dot(lo, spread_map)
 
     decays[me] = jnp.broadcast_to(jnp.exp(last), (8, 128))
-    pl.semaphore_wait(pltpu.get_barrier_semaphore(), SEQ - 1)
+    pl.semaphore_wait(pltpu.get_barrier_semaphore(), 15 + 7 + 1)
 
     def dec_copy(d, there):
         return remote(
@@ -199,44 +198,18 @@
     outer = dot(c_ref[...], entry[...])
     mamba = (y_ref[...] + cum_wide * outer + skip_wide * x_ref[...].astype(F32)).astype(BF16)
     mamba_ref[...] = mamba
-    slots_ref[...] = dot(slot_t, mamba).astype(BF16)
-
-    def wait_sends(d, carry):
-        dec_copy(d, me).wait_send()
-        a_copy(d, me).wait_send()
-        p_copy(d, me).wait_send()
-        return carry
-
-    lax.fori_loop(1, SEQ, wait_sends, 0)
-
-
-def scan_call(*args):
-    vm = pl.BlockSpec(memory_space=pltpu.VMEM)
-    dma = pltpu.SemaphoreType.DMA
-    return pl.pallas_call(
-        scan_kernel,
-        out_shape=(
-            jax.ShapeDtypeStruct((TOK, CH), BF16),
-            jax.ShapeDtypeStruct((CAP, CH), BF16),
-            jax.ShapeDtypeStruct((TOK, 128), BF16),
-        ),
-        in_specs=[vm] * len(args),
-        out_specs=(vm, vm, vm),
-        scratch_shapes=[
-            pltpu.VMEM((128, TOK), F32),
-            pltpu.VMEM((128, CH), BF16),
-            pltpu.VMEM((SEQ, 16, 512), BF16),
-            pltpu.VMEM((SEQ, 8, 128), F32),
-            pltpu.VMEM((SEQ, 16, 512), BF16),
-            pltpu.VMEM((128, CH), BF16),
-            pltpu.VMEM((TOK, CH), F32),
-        ]
-        + [dma((SEQ,))] * 6,
-        compiler_params=pltpu.CompilerParams(
-            collective_id=0, has_side_effects=True, vmem_limit_bytes=VMEM_LIMIT
-        ),
-        name="scan",
-    )(*args)
+    rows[me] = dot(slot_t, mamba).astype(BF16)
+
+    def drain():
+        def wait_sends(d, carry):
+            dec_copy(d, me).wait_send()
+            a_copy(d, me).wait_send()
+            p_copy(d, me).wait_send()
+            return carry
+
+        lax.fori_loop(1, SEQ, wait_sends, 0)
+
+    return drain
 
 
 def near_first(i):
@@ -244,8 +217,8 @@
     return odd * ((i + 1) // 2) + (1 - odd) * ((NZ - i // 2) % NZ)
 
 
-def expert_kernel(
-    slots_ref, rescale_ref, switch_ref, widen_ref, contract_ref,
+def expert_part(
+    idle, rescale_ref, switch_ref, widen_ref, contract_ref,
     out_ref,
     rows, pg, pu, g1, u1, us, g2, u2, hidden, x_out, x_in, kept, z_out, z_in,
     ag_send, ag_recv, fw_send, fw_recv,
@@ -259,22 +232,12 @@
     y, xl = ch // 2, ch % 2
     other = {"seq": (1 - xh) * NZ + z}
     beside = {"chan": y * 2 + 1 - xl}
-    barrier = pltpu.get_barrier_semaphore()
 
     def at_z(there):
         return {"seq": xh * NZ + there % NZ}
 
     def at_y(there):
         return {"chan": (there % 4) * 2 + xl}
-
-    for d in range(1, NZ):
-        pl.semaphore_signal(barrier, inc=1, device_id=at_z(z + d), device_id_type=MESH)
-    for d in range(1, 4):
-        pl.semaphore_signal(barrier, inc=1, device_id=at_y(y + d), device_id_type=MESH)
-    pl.semaphore_signal(barrier, inc=1, device_id=other, device_id_type=MESH)
-    pl.semaphore_signal(barrier, inc=1, device_id=beside, device_id_type=MESH)
-    rows[me] = slots_ref[...]
-    pl.semaphore_wait(barrier, 7 + 3 + 1 + 1)
 
     def order(i):
         return (z - near_first(i) + NZ) % NZ
@@ -308,6 +271,7 @@
             remote(rows.at[(1 - xh) * NZ + z], rows.at[(1 - xh) * NZ + z], fw_send, fw_recv, other).wait_recv()
             for way in range(2):
                 ag_copy(way, 1, 1 - xh, z).start()
+            idle()
 
         @pl.when((i % 2 == 1) & (i < NZ - 1))
         def _():
@@ -459,71 +423,38 @@
 
     lax.fori_loop(1, NZ, collect, 0)
 
-    def wait_sends(b, carry):
-        g1_copy(b).wait_send()
-        u2_copy(b).wait_send()
-        hx_copy(b, xl).wait_send()
-        xs_copy(b).wait_send()
-        for d in range(1, 4):
-            u1_copy(b, d, y, y).wait_send()
-            g2_copy(b, d, y, y).wait_send()
+    def drain():
+        def wait_sends(b, carry):
+            g1_copy(b).wait_send()
+            u2_copy(b).wait_send()
+            hx_copy(b, xl).wait_send()
+            xs_copy(b).wait_send()
+            for d in range(1, 4):
+                u1_copy(b, d, y, y).wait_send()
+                g2_copy(b, d, y, y).wait_send()
+                for half in range(2):
+                    hy_copy(b, half, d, y, y).wait_send()
+            return carry
+
+        lax.fori_loop(0, NZ, wait_sends, 0)
+
+        def wait_z_sends(i, carry):
+            zs_copy(i, z, z).wait_send()
+            return carry
+
+        lax.fori_loop(1, NZ, wait_z_sends, 0)
+        fw.wait_send()
+        for way in range(2):
             for half in range(2):
-                hy_copy(b, half, d, y, y).wait_send()
-        return carry
-
-    lax.fori_loop(0, NZ, wait_sends, 0)
-
-    def wait_z_sends(i, carry):
-        zs_copy(i, z, z).wait_send()
-        return carry
-
-    lax.fori_loop(1, NZ, wait_z_sends, 0)
-    fw.wait_send()
-    for way in range(2):
-        for half in range(2):
-            ag_last(way, half, z).wait_send()
-            for k in range(1, 4):
-                ag_copy(way, k, half, z).wait_send()
-
-
-def expert_call(*args):
-    vm = pl.BlockSpec(memory_space=pltpu.VMEM)
-    dma = pltpu.SemaphoreType.DMA
-    return pl.pallas_call(
-        expert_kernel,
-        out_shape=jax.ShapeDtypeStruct((CAP, CH), F32),
-        in_specs=[vm] * len(args),
-        out_specs=vm,
-        scratch_shapes=[
-            pltpu.VMEM((SEQ, CAP, CH), BF16),
-            pltpu.VMEM((NZ, 2, 64, HIDL + 128), BF16),
-            pltpu.VMEM((NZ, 2, 64, HIDL), BF16),
-            pltpu.VMEM((NZ, 64, HIDL + 128), BF16),
-            pltpu.VMEM((NZ, 4, 2, 16, HIDL), BF16),
-            pltpu.VMEM((NZ, 2, 16, HIDL), BF16),
-            pltpu.VMEM((NZ, 4, 16, HIDL + 128), BF16),
-            pltpu.VMEM((NZ, 16, HIDL), BF16),
-            pltpu.VMEM((NZ, 2, 64, HIDL), BF16),
-            pltpu.VMEM((NZ, CAP, CH), BF16),
-            pltpu.VMEM((NZ, CAP, CH), BF16),
-            pltpu.VMEM((NZ, CAP, CH), F32),
-            pltpu.VMEM((NZ, CAP, CH), BF16),
-            pltpu.VMEM((NZ, CAP, CH), BF16),
-            dma((2, 5, 2)), dma((2, 5, 2)), dma, dma,
-            dma((NZ,)), dma((NZ,)), dma((NZ, 4)), dma((NZ, 4)),
-            dma((NZ, 4)), dma((NZ, 4)), dma((NZ,)), dma((NZ,)),
-            dma((NZ,)), dma((NZ,)), dma((NZ, 2, 4)), dma((NZ, 2, 4)),
-            dma((NZ,)), dma((NZ,)), dma((NZ,)), dma((NZ,)),
-        ],
-        compiler_params=pltpu.CompilerParams(
-            collective_id=1, has_side_effects=True, vmem_limit_bytes=VMEM_LIMIT
-        ),
-        name="expert",
-    )(*args)
-
-
-def head_kernel(
-    mamba_ref, gmap_ref, expert_ref, pick_ref, closing_ref, lexicon_ref, div_ref,
+                ag_last(way, half, z).wait_send()
+                for k in range(1, 4):
+                    ag_copy(way, k, half, z).wait_send()
+
+    return drain
+
+
+def head_part(
+    idle, mamba_ref, gmap_ref, expert_ref, pick_ref, closing_ref, lexicon_ref, div_ref,
     layer_ref, prob_ref,
     held, acc, squares, chan_stats, seq_stats,
     z_send, z_recv, a_send, a_recv, b_send, b_recv, c_send, c_recv, s_send, s_recv,
@@ -533,12 +464,6 @@
     xh, z = me // NZ, me % NZ
     y, xl = ch // 2, ch % 2
     x = xh * 2 + xl
-    barrier = pltpu.get_barrier_semaphore()
-    greet("seq", SEQ, me)
-    greet("chan", CHAN, ch)
-    diagonal = {"seq": (1 - xh) * NZ + z, "chan": y * 2 + 1 - xl}
-    pl.semaphore_signal(barrier, inc=1, device_id=diagonal, device_id_type=MESH)
-
     hi, lo = split2(expert_ref[...])
     gmap = gmap_ref[:, 0:CAP]
     layer = (mamba_ref[...].astype(F32) + dot(gmap, hi) + dot(gmap, lo)).astype(BF16)
@@ -552,8 +477,6 @@
     own = pl.ds(pl.multiple_of(z * 16, 16), 16)
     held[0, y, x, own, :] = picked[:, 0:512]
     held[1, y, x, own, :] = picked[:, 512:1024]
-    pl.semaphore_wait(barrier, 15 + 7 + 1)
-
     def at_x(there):
         return {"seq": (there // 2) * NZ + z, "chan": y * 2 + there % 2}
 
@@ -594,6 +517,7 @@
         second_copy(0, 0, d, y, x, at_x((x + d) % 4)).start()
         second_copy(1, 0, d, y, x, at_y((y + d) % 4)).start()
 
+    idle()
     acc[...] = jnp.zeros_like(acc)
     squares[...] = jnp.zeros_like(squares)
 
@@ -672,6 +596,22 @@
 
     lax.fori_loop(1, SEQ, send_s, 0)
 
+    def wait_sends(d, carry):
+        z_copy(d, z, z).wait_send()
+        chan_copy(d, ch, ch).wait_send()
+        return carry
+
+    lax.fori_loop(1, NZ, wait_sends, 0)
+
+    def wait_a_sends(d, carry):
+        for h in range(2):
+            first_copy(h, d, y, x, at_y(y)).wait_send()
+            for k in range(4):
+                second_copy(h, k, d, y, x, at_y(y)).wait_send()
+        return carry
+
+    lax.fori_loop(1, 4, wait_a_sends, 0)
+
     def wait_s(d, carry):
         seq_copy(d, lax.rem(me - d + SEQ, SEQ), me).wait_recv()
         return carry
@@ -682,41 +622,104 @@
     column = jnp.transpose(jnp.broadcast_to(norm[0:1, :], (128, TOK)))[:, 0:1]
     prob_ref[...] = scores - column
 
-    def wait_sends(d, carry):
-        z_copy(d, z, z).wait_send()
-        chan_copy(d, ch, ch).wait_send()
-        return carry
-
-    lax.fori_loop(1, NZ, wait_sends, 0)
-
     def wait_s_sends(d, carry):
         seq_copy(d, me, me).wait_send()
         return carry
 
     lax.fori_loop(1, SEQ, wait_s_sends, 0)
 
-    def wait_a_sends(d, carry):
-        for h in range(2):
-            first_copy(h, d, y, x, at_y(y)).wait_send()
-            for k in range(4):
-                second_copy(h, k, d, y, x, at_y(y)).wait_send()
-        return carry
-
-    lax.fori_loop(1, 4, wait_a_sends, 0)
-
-
-def head_call(*args):
+
+def whole_kernel(
+    x_ref, b_ref, c_ref, la_ref, skip_ref, choice_ref, share_ref,
+    rescale_ref, switch_hbm, widen_hbm, contract_hbm,
+    pick_ref, closing_ref, lexicon_hbm, div_ref,
+    layer_ref, prob_ref,
+    mamba, gmap, expert, switch, widen, contract, lexicon, rows, load_sem,
+    *scratch,
+):
+    barrier = pltpu.get_barrier_semaphore()
+    me = lax.axis_index("seq")
+    ch = lax.axis_index("chan")
+    greet("seq", SEQ, me)
+    greet("chan", CHAN, ch)
+    xh, z = me // NZ, me % NZ
+    y, xl = ch // 2, ch % 2
+    diagonal = {"seq": (1 - xh) * NZ + z, "chan": y * 2 + 1 - xl}
+    pl.semaphore_signal(barrier, inc=1, device_id=diagonal, device_id_type=MESH)
+    loads = [
+        pltpu.make_async_copy(src, dst, load_sem.at[k])
+        for k, (src, dst) in enumerate(
+            ((switch_hbm, switch), (widen_hbm, widen), (contract_hbm, contract), (lexicon_hbm, lexicon))
+        )
+    ]
+    for load in loads:
+        load.start()
+    drain = scan_part(
+        x_ref, b_ref, c_ref, la_ref, skip_ref, choice_ref, share_ref,
+        mamba, rows, gmap, *scratch[:13],
+    )
+    first = drain
+
+    def idle():
+        first()
+        for load in loads:
+            load.wait()
+
+    drain = expert_part(idle, rescale_ref, switch, widen, contract, expert, rows, *scratch[13 : 13 + 33])
+    head_part(
+        drain, mamba, gmap, expert, pick_ref, closing_ref, lexicon, div_ref, layer_ref, prob_ref, *scratch[46:]
+    )
+
+
+def whole_call(*args):
     vm = pl.BlockSpec(memory_space=pltpu.VMEM)
+    hbm = pl.BlockSpec(memory_space=pl.ANY)
     dma = pltpu.SemaphoreType.DMA
+    in_specs = [vm] * 8 + [hbm] * 3 + [vm] * 2 + [hbm, pl.BlockSpec(memory_space=pltpu.SMEM)]
     return pl.pallas_call(
-        head_kernel,
+        whole_kernel,
         out_shape=(
             jax.ShapeDtypeStruct((TOK, CH), BF16),
             jax.ShapeDtypeStruct((TOK, TOK), F32),
         ),
-        in_specs=[vm] * (len(args) - 1) + [pl.BlockSpec(memory_space=pltpu.SMEM)],
+        in_specs=in_specs,
         out_specs=(vm, vm),
         scratch_shapes=[
+            pltpu.VMEM((TOK, CH), BF16),
+            pltpu.VMEM((TOK, 128), BF16),
+            pltpu.VMEM((CAP, CH), F32),
+            pltpu.VMEM((CH, HIDL), BF16),
+            pltpu.VMEM((CH, HIDL), BF16),
+            pltpu.VMEM((HIDL, CH), BF16),
+            pltpu.VMEM((WIDTH, TOK), BF16),
+            pltpu.VMEM((SEQ, CAP, CH), BF16),
+            dma((4,)),
+            pltpu.VMEM((128, TOK), F32),
+            pltpu.VMEM((128, CH), BF16),
+            pltpu.VMEM((SEQ, 16, 512), BF16),
+            pltpu.VMEM((SEQ, 8, 128), F32),
+            pltpu.VMEM((SEQ, 16, 512), BF16),
+            pltpu.VMEM((128, CH), BF16),
+            pltpu.VMEM((TOK, CH), F32),
+            *[dma((SEQ,))] * 6,
+            pltpu.VMEM((NZ, 2, 64, HIDL + 128), BF16),
+            pltpu.VMEM((NZ, 2, 64, HIDL), BF16),
+            pltpu.VMEM((NZ, 64, HIDL + 128), BF16),
+            pltpu.VMEM((NZ, 4, 2, 16, HIDL), BF16),
+            pltpu.VMEM((NZ, 2, 16, HIDL), BF16),
+            pltpu.VMEM((NZ, 4, 16, HIDL + 128), BF16),
+            pltpu.VMEM((NZ, 16, HIDL), BF16),
+            pltpu.VMEM((NZ, 2, 64, HIDL), BF16),
+            pltpu.VMEM((NZ, CAP, CH), BF16),
+            pltpu.VMEM((NZ, CAP, CH), BF16),
+            pltpu.VMEM((NZ, CAP, CH), F32),
+            pltpu.VMEM((NZ, CAP, CH), BF16),
+            pltpu.VMEM((NZ, CAP, CH), BF16),
+            dma((2, 5, 2)), dma((2, 5, 2)), dma, dma,
+            dma((NZ,)), dma((NZ,)), dma((NZ, 4)), dma((NZ, 4)),
+            dma((NZ, 4)), dma((NZ, 4)), dma((NZ,)), dma((NZ,)),
+            dma((NZ,)), dma((NZ,)), dma((NZ, 2, 4)), dma((NZ, 2, 4)),
+            dma((NZ,)), dma((NZ,)), dma((NZ,)), dma((NZ,)),
             pltpu.VMEM((2, 4, 4, 128, 512), BF16),
             pltpu.VMEM((2, 128, TOK), F32),
             pltpu.VMEM((2, 128, 1), F32),
@@ -729,9 +732,9 @@
             dma((SEQ,)), dma((SEQ,)),
         ],
         compiler_params=pltpu.CompilerParams(
-            collective_id=2, has_side_effects=True, vmem_limit_bytes=VMEM_LIMIT
+            collective_id=0, has_side_effects=True, vmem_limit_bytes=VMEM_LIMIT
         ),
-        name="head",
+        name="whole",
     )(*args)
 
 
@@ -752,7 +755,7 @@
     softness_divisor,
     picked_entry_offsets,
 ):
-    mamba, slots, gmap = scan_call(
+    return whole_call(
         recurrence_feed,
         memory_write_matrix,
         memory_read_matrix,
@@ -760,18 +763,10 @@
         skip_connection_scale.reshape(1, -1),
         specialist_choices.T,
         specialist_mixing_shares.T,
-    )
-    expert = expert_call(
-        slots,
         specialist_rescale_vector.reshape(1, -1),
         specialist_switch_matrix,
         specialist_widen_matrix,
         specialist_contract_matrix,
-    )
-    return head_call(
-        mamba,
-        gmap,
-        expert,
         picked_entry_offsets.reshape(1, -1),
         closing_rescale_vector.reshape(1, -1),
         lexicon_matrix,

time: 181 us -> 166 us (0.917)
  Pallas kernels: 175 us -> 161 us
    pallas_call x3 -> x1, Pallas kernels: 175 us -> 161 us  [whole_call(): pl.pallas_call(whole_kernel, out_shape=(jax.ShapeDtypeStruct((TOK, CH), B...]
where the time goes in v3:
time: 166 us
  Pallas kernels  161 us (97%)
  local copies, waits for them, and re-layouts  3.54 us (2%)
    pallas_call x1, Pallas kernels, whole_call(): pl.pallas_call(whole_kernel, out_shape=(jax.ShapeDtypeStruct((TOK, CH), B...  161 us
    unnamed x2, local copies, waits for them, and re-layouts  3.54 us

profile of v3, /device:TPU:2, one launch (start us, length us, event | category | flops | bytes accessed | tf_op | source)
XLA Modules:
  0.0 166.1 jit_solution(3330042961148611527)
XLA Ops:
  1.3 161.3 %whole.1 = (bf16[256,1024]{1,0:T(8,128)(2,1)}, f32[256,256]{1,0:T(8,128)}) custom-call(bf16[256,1024]{1,0:T(8,128)(2,1)} %x_ref.1, bf16[256,128]{1,0:T(8,128)(2,1)} %b_ref.1, bf16[256,128]{1,0:T(8,128)(2,1)} %c_ref.1, f32[16,256]{1,0:T(8,128)} %bitcast.10, f32[1,16]{1,0:T(1,128)} %bitcast.14, s32[2,256]{1,0:T(2,128)} %bitcast.12, bf16[2,256]{1,0:T(2,128)(2,1)} %bitcast.13, ...), custom_call_target="tpu_custom_call" | custom-call | tf_op jit(solution)/shard_map/whole/pallas_call | solution.py:679
  162.6 1.9 %copy.20 = bf16[256,1024]{1,0:T(8,128)(2,1)} copy(bf16[256,1024]{1,0:T(8,128)(2,1)} %get-tuple-element.4) | data formatting | bytes 1048576
  164.4 1.7 %copy.21 = f32[256,256]{1,0:T(8,128)} copy(f32[256,256]{1,0:T(8,128)} %get-tuple-element.5) | data formatting | bytes 524288

commit v4 on v3

--- a/solution.py
+++ b/solution.py
@@ -185,7 +185,17 @@
 
     skip = jnp.concatenate([skip_ref[...], jnp.zeros((1, 112), F32)], axis=1)
     skip_wide = expand(jnp.broadcast_to(skip, (8, 128)))[0:1, :]
-    cum_wide = expand(jnp.exp(cum))
+    decay_in = jnp.exp(cum)
+    cum_wide = expand(decay_in)
+    y_ref[...] += skip_wide * x_ref[...].astype(F32)
+
+    def routed(v):
+        hi, mid, lo = split3(v)
+        return dot(slot_t, hi) + dot(slot_t, mid) + dot(slot_t, lo)
+
+    slot_before = routed(y_ref[...])
+    slot_cum = expand(routed(decay_in))
+    slot_c = dot(slot_t, c_ref[...]).astype(BF16)
 
     def wait_p(d, carry):
         there = lax.rem(me - d + SEQ, SEQ)
@@ -195,10 +205,11 @@
         return carry
 
     lax.fori_loop(1, SEQ, wait_p, 0)
-    outer = dot(c_ref[...], entry[...])
-    mamba = (y_ref[...] + cum_wide * outer + skip_wide * x_ref[...].astype(F32)).astype(BF16)
-    mamba_ref[...] = mamba
-    rows[me] = dot(slot_t, mamba).astype(BF16)
+    rows[me] = (slot_before + slot_cum * dot(slot_c, entry[...])).astype(BF16)
+
+    def finish():
+        outer = dot(c_ref[...], entry[...])
+        mamba_ref[...] = (y_ref[...] + cum_wide * outer).astype(BF16)
 
     def drain():
         def wait_sends(d, carry):
@@ -209,7 +220,7 @@
 
         lax.fori_loop(1, SEQ, wait_sends, 0)
 
-    return drain
+    return drain, finish
 
 
 def near_first(i):
@@ -218,7 +229,7 @@
 
 
 def expert_part(
-    idle, rescale_ref, switch_ref, widen_ref, contract_ref,
+    finish, idle, rescale_ref, switch_ref, widen_ref, contract_ref,
     out_ref,
     rows, pg, pu, g1, u1, us, g2, u2, hidden, x_out, x_in, kept, z_out, z_in,
     ag_send, ag_recv, fw_send, fw_recv,
@@ -264,6 +275,7 @@
     fw.start()
     for way in range(2):
         ag_copy(way, 1, xh, z).start()
+    finish()
 
     def gather(i):
         @pl.when(i == 0)
@@ -456,8 +468,8 @@
 def head_part(
     idle, mamba_ref, gmap_ref, expert_ref, pick_ref, closing_ref, lexicon_ref, div_ref,
     layer_ref, prob_ref,
-    held, acc, squares, chan_stats, seq_stats,
-    z_send, z_recv, a_send, a_recv, b_send, b_recv, c_send, c_recv, s_send, s_recv,
+    held, acc, ordered, squares, chan_stats, seq_stats,
+    z_send, z_recv, r_send, r_recv, c_send, c_recv, s_send, s_recv,
 ):
     me = lax.axis_index("seq")
     ch = lax.axis_index("chan")
@@ -474,90 +486,120 @@
     offsets = jnp.transpose(jnp.broadcast_to(offsets, (128, 128)))[0:16, 0:1]
     pick = (iota((16, TOK), 1).astype(F32) == offsets).astype(F32).astype(BF16)
     picked = dot(pick, layer).astype(BF16)
-    own = pl.ds(pl.multiple_of(z * 16, 16), 16)
-    held[0, y, x, own, :] = picked[:, 0:512]
-    held[1, y, x, own, :] = picked[:, 512:1024]
+    held[0, y, x, 0:16, :] = picked[:, 0:512]
+    held[1, y, x, 0:16, :] = picked[:, 512:1024]
+
     def at_x(there):
+        there = there % 4
         return {"seq": (there // 2) * NZ + z, "chan": y * 2 + there % 2}
 
     def at_y(there):
-        return {"chan": there * 2 + xl}
-
-    def z_copy(d, source, there):
-        ref = held.at[:, y, x, pl.ds(pl.multiple_of(source * 16, 16), 16), :]
-        return remote(ref, ref, z_send.at[d], z_recv.at[d], {"seq": xh * NZ + there})
-
-    def send_z(i, carry):
-        d = near_first(i)
-        z_copy(d, z, (z + d) % NZ).start()
-        return carry
-
-    lax.fori_loop(1, NZ, send_z, 0)
-
-    def piece(h, yy, xx):
-        return held.at[h, yy, xx]
-
-    def first_copy(h, d, yy, xx, there):
-        ref = piece(h, yy, xx)
-        return remote(ref, ref, a_send.at[h, d], a_recv.at[h, d], there)
-
-    def second_copy(h, k, d, yy, xx, there):
-        ref = piece(h, yy, xx)
-        return remote(ref, ref, b_send.at[h, k, d], b_recv.at[h, k, d], there)
-
-    def wait_z(d, carry):
-        z_copy(d, (z - d + NZ) % NZ, z).wait_recv()
-        return carry
-
-    lax.fori_loop(1, NZ, wait_z, 0)
-    for d in (1, 3, 2):
-        first_copy(0, d, y, x, at_y((y + d) % 4)).start()
-        first_copy(1, d, y, x, at_x((x + d) % 4)).start()
-    for d in (1, 3, 2):
-        second_copy(0, 0, d, y, x, at_x((x + d) % 4)).start()
-        second_copy(1, 0, d, y, x, at_y((y + d) % 4)).start()
-
-    idle()
+        return {"chan": (there % 4) * 2 + xl}
+
+    def z_copy(r):
+        return remote(
+            held.at[:, y, x, pl.ds(0, 16), :],
+            held.at[:, y, x, pl.ds(16 * r, 16), :],
+            z_send.at[r],
+            z_recv.at[r],
+            {"seq": xh * NZ + (z + near_first(r)) % NZ},
+        )
+
+    for r in range(1, NZ):
+        z_copy(r).start()
+
+    def piece(h, stage, e, g, kind):
+        k, e = (e, 0) if stage == 0 else (stage - 1, e)
+        yy, xx = (k, e) if h == 0 else (e, k)
+        rows = (pl.ds(64 * g, 64), pl.ds(64 * g, 64), pl.ds(64 * g, 32), pl.ds(64 * g + 32, 32))[kind]
+        return held.at[h, (y - yy + 4) % 4, (x - xx + 4) % 4, rows]
+
+    def ring(h, stage, g, kind, source):
+        ref = piece(h, stage, source, g, kind)
+        move = 1 if kind % 2 == 0 else 3
+        there = at_y(y + move) if (h == 0) == (stage == 0) else at_x(x + move)
+        return remote(ref, ref, r_send.at[h, stage, g, kind], r_recv.at[h, stage, g, kind], there)
+
+    def start(stage, g):
+        for h in range(2):
+            for kind in range(2):
+                ring(h, stage, g, kind, 0).start()
+
+    def arrive(stage, g):
+        for kind in range(2):
+            for h in range(2):
+                ring(h, stage, g, kind, (1, 3)[kind]).wait_recv()
+                ring(h, stage, g, kind + 2, (1, 3)[kind]).start()
+
+    def arrive_far(stage, g):
+        for h in range(2):
+            for kind in (2, 3):
+                ring(h, stage, g, kind, 2).wait_recv()
+
     acc[...] = jnp.zeros_like(acc)
     squares[...] = jnp.zeros_like(squares)
 
-    def use(h, yy, xx):
-        upper, right = xx // 2, xx % 2
-        first = pl.multiple_of((yy * 2 + right) * CH + h * 512, 512)
-        v = held[h, yy, xx].astype(F32)
-        squares[upper] += jnp.sum(v * v, axis=1, keepdims=True)
-        scaled = (v * closing_ref[:, pl.ds(first, 512)]).astype(BF16)
-        acc[upper] += dot(scaled, lexicon_ref[pl.ds(first, 512), :])
-
-    def own_pieces(h, carry):
-        use(h, y, x)
-        return carry
-
-    lax.fori_loop(0, 2, own_pieces, 0)
-    for d in (1, 3, 2):
-        yy, xx = (y - d + 4) % 4, (x - d + 4) % 4
-        first_copy(0, d, yy, x, at_y(y)).wait_recv()
-        first_copy(1, d, y, xx, at_x(x)).wait_recv()
-        for e in (1, 3, 2):
-            second_copy(0, d, e, yy, x, at_x((x + e) % 4)).start()
-            second_copy(1, d, e, y, xx, at_y((y + e) % 4)).start()
-    for d in (1, 3, 2):
-        use(0, (y - d + 4) % 4, x)
-        use(1, y, (x - d + 4) % 4)
-    def last_pieces(k, carry):
-        for e in (1, 3, 2):
-            yy, xx = (y - k + 4) % 4, (x - e + 4) % 4
-            second_copy(0, k, e, yy, xx, at_x(x)).wait_recv()
-            use(0, yy, xx)
-            yy, xx = (y - e + 4) % 4, (x - k + 4) % 4
-            second_copy(1, k, e, yy, xx, at_y(y)).wait_recv()
-            use(1, yy, xx)
-        return carry
-
-    lax.fori_loop(0, 4, last_pieces, 0)
-
-    inv = lax.rsqrt(squares[...] / WIDTH + EPS).reshape(TOK, 1)
-    scores = acc[...].reshape(TOK, TOK) * inv / div_ref[0, 0]
+    def use(stage, e):
+        for h in range(2):
+            k, ee = (e, 0) if stage == 0 else (stage - 1, e)
+            yy, xx = (k, ee) if h == 0 else (ee, k)
+            yy, xx = (y - yy + 4) % 4, (x - xx + 4) % 4
+            upper, right = xx // 2, xx % 2
+            first = pl.multiple_of((yy * 2 + right) * CH + h * 512, 512)
+            v = held[h, yy, xx].astype(F32)
+            squares[upper] += jnp.sum(v * v, axis=1, keepdims=True)
+            scaled = (v * closing_ref[:, pl.ds(first, 512)]).astype(BF16)
+            acc[upper] += dot(scaled, lexicon_ref[pl.ds(first, 512), :])
+
+    for r in range(1, 4):
+        z_copy(r).wait_recv()
+    start(0, 0)
+    start(1, 0)
+    for r in range(4, NZ):
+        z_copy(r).wait_recv()
+    start(0, 1)
+    start(1, 1)
+    use(0, 0)
+    idle()
+    for g in range(2):
+        arrive(0, g)
+        for k in (1, 3):
+            start(1 + k, g)
+        arrive(1, g)
+    for g in range(2):
+        arrive_far(0, g)
+        start(3, g)
+    for e in (1, 3, 2):
+        use(0, e)
+    for e in (1, 3):
+        use(1, e)
+    for g in range(2):
+        for k in (1, 3):
+            arrive(1 + k, g)
+    for g in range(2):
+        arrive_far(1, g)
+    use(1, 2)
+    for k in (1, 3):
+        for e in (1, 3):
+            use(1 + k, e)
+    for g in range(2):
+        arrive(3, g)
+    for k in (1, 3):
+        for g in range(2):
+            arrive_far(1 + k, g)
+        use(1 + k, 2)
+    for e in (1, 3):
+        use(3, e)
+    for g in range(2):
+        arrive_far(3, g)
+    use(3, 2)
+
+    inv = lax.rsqrt(squares[...] / WIDTH + EPS)
+    for r in range(NZ):
+        rows = pl.ds(pl.multiple_of(((z - near_first(r) + NZ) % NZ) * 16, 16), 16)
+        part = slice(16 * r, 16 * r + 16)
+        ordered[:, rows, :] = acc[:, part, :] * inv[:, part, :]
+    scores = ordered[...].reshape(TOK, TOK) / div_ref[0, 0]
     top = jnp.max(scores, axis=1, keepdims=True)
     mass = jnp.sum(jnp.exp(scores - top), axis=1, keepdims=True)
     chan_stats[ch, 0] = jnp.transpose(jnp.broadcast_to(top, (TOK, 128)))[0:8, :]
@@ -597,20 +639,16 @@
     lax.fori_loop(1, SEQ, send_s, 0)
 
     def wait_sends(d, carry):
-        z_copy(d, z, z).wait_send()
+        z_copy(d).wait_send()
         chan_copy(d, ch, ch).wait_send()
         return carry
 
     lax.fori_loop(1, NZ, wait_sends, 0)
-
-    def wait_a_sends(d, carry):
-        for h in range(2):
-            first_copy(h, d, y, x, at_y(y)).wait_send()
-            for k in range(4):
-                second_copy(h, k, d, y, x, at_y(y)).wait_send()
-        return carry
-
-    lax.fori_loop(1, 4, wait_a_sends, 0)
+    for stage in range(5):
+        for g in range(2):
+            for h in range(2):
+                for kind in range(4):
+                    ring(h, stage, g, kind, 0).wait_send()
 
     def wait_s(d, carry):
         seq_copy(d, lax.rem(me - d + SEQ, SEQ), me).wait_recv()
@@ -654,18 +692,16 @@
     ]
     for load in loads:
         load.start()
-    drain = scan_part(
+    first, finish = scan_part(
         x_ref, b_ref, c_ref, la_ref, skip_ref, choice_ref, share_ref,
         mamba, rows, gmap, *scratch[:13],
     )
-    first = drain
-
     def idle():
         first()
         for load in loads:
             load.wait()
 
-    drain = expert_part(idle, rescale_ref, switch, widen, contract, expert, rows, *scratch[13 : 13 + 33])
+    drain = expert_part(finish, idle, rescale_ref, switch, widen, contract, expert, rows, *scratch[13 : 13 + 33])
     head_part(
         drain, mamba, gmap, expert, pick_ref, closing_ref, lexicon, div_ref, layer_ref, prob_ref, *scratch[46:]
     )
@@ -722,12 +758,12 @@
             dma((NZ,)), dma((NZ,)), dma((NZ,)), dma((NZ,)),
             pltpu.VMEM((2, 4, 4, 128, 512), BF16),
             pltpu.VMEM((2, 128, TOK), F32),
+            pltpu.VMEM((2, 128, TOK), F32),
             pltpu.VMEM((2, 128, 1), F32),
             pltpu.VMEM((CHAN, 2, 8, TOK), F32),
             pltpu.VMEM((SEQ, 2, 8, TOK), F32),
             dma((NZ,)), dma((NZ,)),
-            dma((2, 4)), dma((2, 4)),
-            dma((2, 4, 4)), dma((2, 4, 4)),
+            dma((2, 5, 2, 4)), dma((2, 5, 2, 4)),
             dma((CHAN,)), dma((CHAN,)),
             dma((SEQ,)), dma((SEQ,)),
         ],

time: 166 us -> 158 us (0.952)
  Pallas kernels: 161 us -> 153 us
    pallas_call x1, Pallas kernels: 161 us -> 153 us  [whole_call(): pl.pallas_call(whole_kernel, out_shape=(jax.ShapeDtypeStruct((TOK, CH), B...]
where the time goes in v4:
time: 158 us
  Pallas kernels  153 us (97%)
  local copies, waits for them, and re-layouts  3.54 us (2%)
    pallas_call x1, Pallas kernels, whole_call(): pl.pallas_call(whole_kernel, out_shape=(jax.ShapeDtypeStruct((TOK, CH), B...  153 us
    unnamed x2, local copies, waits for them, and re-layouts  3.54 us

profile of v4, /device:TPU:2, one launch (start us, length us, event | category | flops | bytes accessed | tf_op | source)
XLA Modules:
  0.0 158.3 jit_solution(1182708990486733693)
XLA Ops:
  1.3 153.5 %whole.1 = (bf16[256,1024]{1,0:T(8,128)(2,1)}, f32[256,256]{1,0:T(8,128)}) custom-call(bf16[256,1024]{1,0:T(8,128)(2,1)} %x_ref.1, bf16[256,128]{1,0:T(8,128)(2,1)} %b_ref.1, bf16[256,128]{1,0:T(8,128)(2,1)} %c_ref.1, f32[16,256]{1,0:T(8,128)} %bitcast.10, f32[1,16]{1,0:T(1,128)} %bitcast.14, s32[2,256]{1,0:T(2,128)} %bitcast.12, bf16[2,256]{1,0:T(2,128)(2,1)} %bitcast.13, ...), custom_call_target="tpu_custom_call" | custom-call | tf_op jit(solution)/shard_map/whole/pallas_call | solution.py:715
  154.8 1.9 %copy.20 = bf16[256,1024]{1,0:T(8,128)(2,1)} copy(bf16[256,1024]{1,0:T(8,128)(2,1)} %get-tuple-element.4) | data formatting | bytes 1048576
  156.6 1.7 %copy.21 = f32[256,256]{1,0:T(8,128)} copy(f32[256,256]{1,0:T(8,128)} %get-tuple-element.5) | data formatting | bytes 524288

commit v5 on v4

--- a/solution.py
+++ b/solution.py
@@ -602,8 +602,15 @@
     scores = ordered[...].reshape(TOK, TOK) / div_ref[0, 0]
     top = jnp.max(scores, axis=1, keepdims=True)
     mass = jnp.sum(jnp.exp(scores - top), axis=1, keepdims=True)
-    chan_stats[ch, 0] = jnp.transpose(jnp.broadcast_to(top, (TOK, 128)))[0:8, :]
-    chan_stats[ch, 1] = jnp.transpose(jnp.broadcast_to(mass, (TOK, 128)))[0:8, :]
+    tops = jnp.transpose(jnp.broadcast_to(top, (TOK, 128)))[0:8, :]
+    masses = jnp.transpose(jnp.broadcast_to(mass, (TOK, 128)))[0:8, :]
+    row = iota((8, 128), 0)
+    chan_stats[ch] = jnp.where(
+        row == 0,
+        tops[:, 0:128],
+        jnp.where(row == 1, tops[:, 128:256], jnp.where(row == 2, masses[:, 0:128], masses[:, 128:256])),
+    )
+    seq_stats[me] = jnp.zeros((8, 128), F32)
 
     def chan_copy(d, source, there):
         ref = chan_stats.at[source]
@@ -622,11 +629,11 @@
     lax.fori_loop(1, CHAN, wait_c, 0)
 
     def join(ref):
-        tops = ref[:, 0]
+        tops = ref[:, 0:2, :]
         top = jnp.max(tops, axis=0)
-        return top, jnp.sum(ref[:, 1] * jnp.exp(tops - top[None]), axis=0)
-
-    seq_stats[me, 0], seq_stats[me, 1] = join(chan_stats)
+        return top, jnp.sum(ref[:, 2:4, :] * jnp.exp(tops - top[None]), axis=0)
+
+    seq_stats[me, 0:2, :], seq_stats[me, 2:4, :] = join(chan_stats)
 
     def seq_copy(d, source, there):
         ref = seq_stats.at[source]
@@ -657,8 +664,10 @@
     lax.fori_loop(1, SEQ, wait_s, 0)
     top, mass = join(seq_stats)
     norm = top + jnp.log(mass)
-    column = jnp.transpose(jnp.broadcast_to(norm[0:1, :], (128, TOK)))[:, 0:1]
-    prob_ref[...] = scores - column
+    for half in range(2):
+        rows = slice(128 * half, 128 * half + 128)
+        column = jnp.transpose(jnp.broadcast_to(norm[half : half + 1, :], (128, 128)))[:, 0:1]
+        prob_ref[rows, :] = scores[rows, :] - column
 
     def wait_s_sends(d, carry):
         seq_copy(d, me, me).wait_send()
@@ -760,8 +769,8 @@
             pltpu.VMEM((2, 128, TOK), F32),
             pltpu.VMEM((2, 128, TOK), F32),
             pltpu.VMEM((2, 128, 1), F32),
-            pltpu.VMEM((CHAN, 2, 8, TOK), F32),
-            pltpu.VMEM((SEQ, 2, 8, TOK), F32),
+            pltpu.VMEM((CHAN, 8, 128), F32),
+            pltpu.VMEM((SEQ, 8, 128), F32),
             dma((NZ,)), dma((NZ,)),
             dma((2, 5, 2, 4)), dma((2, 5, 2, 4)),
             dma((CHAN,)), dma((CHAN,)),

time: 158 us -> 156 us (0.987)
  Pallas kernels: 153 us -> 151 us
    pallas_call x1, Pallas kernels: 153 us -> 151 us  [whole_call(): pl.pallas_call(whole_kernel, out_shape=(jax.ShapeDtypeStruct((TOK, CH), B...]
where the time goes in v5:
time: 156 us
  Pallas kernels  151 us (97%)
  local copies, waits for them, and re-layouts  3.54 us (2%)
    pallas_call x1, Pallas kernels, whole_call(): pl.pallas_call(whole_kernel, out_shape=(jax.ShapeDtypeStruct((TOK, CH), B...  151 us
    unnamed x2, local copies, waits for them, and re-layouts  3.54 us

profile of v5, /device:TPU:2, one launch (start us, length us, event | category | flops | bytes accessed | tf_op | source)
XLA Modules:
  0.0 155.6 jit_solution(4197831553309313590)
XLA Ops:
  1.3 150.8 %whole.1 = (bf16[256,1024]{1,0:T(8,128)(2,1)}, f32[256,256]{1,0:T(8,128)}) custom-call(bf16[256,1024]{1,0:T(8,128)(2,1)} %x_ref.1, bf16[256,128]{1,0:T(8,128)(2,1)} %b_ref.1, bf16[256,128]{1,0:T(8,128)(2,1)} %c_ref.1, f32[16,256]{1,0:T(8,128)} %bitcast.10, f32[1,16]{1,0:T(1,128)} %bitcast.14, s32[2,256]{1,0:T(2,128)} %bitcast.12, bf16[2,256]{1,0:T(2,128)(2,1)} %bitcast.13, ...), custom_call_target="tpu_custom_call" | custom-call | tf_op jit(solution)/shard_map/whole/pallas_call | solution.py:724
  152.1 1.9 %copy.20 = bf16[256,1024]{1,0:T(8,128)(2,1)} copy(bf16[256,1024]{1,0:T(8,128)(2,1)} %get-tuple-element.4) | data formatting | bytes 1048576
  153.9 1.7 %copy.21 = f32[256,256]{1,0:T(8,128)} copy(f32[256,256]{1,0:T(8,128)} %get-tuple-element.5) | data formatting | bytes 524288

commit v6 on v5

--- a/solution.py
+++ b/solution.py
@@ -536,6 +536,12 @@
             for kind in (2, 3):
                 ring(h, stage, g, kind, 2).wait_recv()
 
+    def sent(stage):
+        for g in range(2):
+            for h in range(2):
+                for kind in range(4):
+                    ring(h, stage, g, kind, 0).wait_send()
+
     acc[...] = jnp.zeros_like(acc)
     squares[...] = jnp.zeros_like(squares)
 
@@ -560,7 +566,6 @@
     start(0, 1)
     start(1, 1)
     use(0, 0)
-    idle()
     for g in range(2):
         arrive(0, g)
         for k in (1, 3):
@@ -569,6 +574,7 @@
     for g in range(2):
         arrive_far(0, g)
         start(3, g)
+    idle()
     for e in (1, 3, 2):
         use(0, e)
     for e in (1, 3):
@@ -588,6 +594,8 @@
         for g in range(2):
             arrive_far(1 + k, g)
         use(1 + k, 2)
+    for stage in (0, 1, 2, 4):
+        sent(stage)
     for e in (1, 3):
         use(3, e)
     for g in range(2):
@@ -651,11 +659,7 @@
         return carry
 
     lax.fori_loop(1, NZ, wait_sends, 0)
-    for stage in range(5):
-        for g in range(2):
-            for h in range(2):
-                for kind in range(4):
-                    ring(h, stage, g, kind, 0).wait_send()
+    sent(3)
 
     def wait_s(d, carry):
         seq_copy(d, lax.rem(me - d + SEQ, SEQ), me).wait_recv()

time: 156 us -> 156 us (level)
  no operation moved by 1% of the time
where the time goes in v6:
time: 156 us
  Pallas kernels  151 us (97%)
  local copies, waits for them, and re-layouts  3.54 us (2%)
    pallas_call x1, Pallas kernels, whole_call(): pl.pallas_call(whole_kernel, out_shape=(jax.ShapeDtypeStruct((TOK, CH), B...  151 us
    unnamed x2, local copies, waits for them, and re-layouts  3.54 us

profile of v6, /device:TPU:2, one launch (start us, length us, event | category | flops | bytes accessed | tf_op | source)
XLA Modules:
  0.0 155.6 jit_solution(14591904565802051128)
XLA Ops:
  1.3 150.8 %whole.1 = (bf16[256,1024]{1,0:T(8,128)(2,1)}, f32[256,256]{1,0:T(8,128)}) custom-call(bf16[256,1024]{1,0:T(8,128)(2,1)} %x_ref.1, bf16[256,128]{1,0:T(8,128)(2,1)} %b_ref.1, bf16[256,128]{1,0:T(8,128)(2,1)} %c_ref.1, f32[16,256]{1,0:T(8,128)} %bitcast.10, f32[1,16]{1,0:T(1,128)} %bitcast.14, s32[2,256]{1,0:T(2,128)} %bitcast.12, bf16[2,256]{1,0:T(2,128)(2,1)} %bitcast.13, ...), custom_call_target="tpu_custom_call" | custom-call | tf_op jit(solution)/shard_map/whole/pallas_call | solution.py:728
  152.1 1.9 %copy.20 = bf16[256,1024]{1,0:T(8,128)(2,1)} copy(bf16[256,1024]{1,0:T(8,128)(2,1)} %get-tuple-element.4) | data formatting | bytes 1048576
  153.9 1.7 %copy.21 = f32[256,256]{1,0:T(8,128)} copy(f32[256,256]{1,0:T(8,128)} %get-tuple-element.5) | data formatting | bytes 524288
